TPU v7x, 32 devices: a whole 2x2x4 slice. The times are simulated.
32 devices in a mesh: dp: 8 (over y, x, core), neg: 4 (over z).
Axes of the slice: x: 2, y: 2, z: 4, core: 2. Of those that a mesh axis runs over, the one named last changes fastest.
Arguments:
- queries: bfloat16 [4096, 4096], P('dp'), may hold values from -144 to 144, as said below
- passages: bfloat16 [8192, 4096], P(('dp', 'neg')), may hold values from -6 to 6
- list_owner: int32 [4, 1024, 1], P('neg', 'dp'), may hold values from 0 to 31; in each aligned block of 128 rows (0 to 127, 128 to 255, ..., all dimensions but the last counted through in order) at most 8 rows name the same one
- list_row: int32 [4, 1024], P('neg', 'dp'), may hold values from 0 to 255
- positive: int32 [4096], P('dp'), may hold values from 0 to 4095
- row_weight: float32 [4096], P('dp'), may hold values from 8 to 32
Outputs:
- query_grad: bfloat16 [4096, 4096], P('dp', 'neg')
- passage_grad: float32 [8192, 4096], P(('dp', 'neg'))
Inputs may be any that keep to these rules, and one draw needn't show every extreme that they name: `queries`: queries are embedding activations. `list_owner`: among the 128 entries of one device no owner appears more than 8 times, and in every draw some device names some owner exactly 8 times.
All inputs are finite; a program needn't handle non-finite values.
Results may differ from a plain program's by a relative error of at most 0.015.
Values may be sent and summed in bfloat16 or wider, within the bound.
No kernel may reach another device: no remote copies, remote signals or barrier semaphores. Data moves between devices by JAX's collectives and lax.ppermute only.
A program may use at most 192 MiB of HBM per device.

v0:
```python
import math

import jax
import jax.numpy as jnp
from jax import lax
from jax.sharding import PartitionSpec as P


def body(queries, passages, list_owner, list_row, positive, row_weight):
    owners = list_owner.reshape(-1)
    row_ids = list_row.reshape(-1)
    list_len = owners.shape[0]
    width = queries.shape[1]
    dp_size = lax.axis_size("dp")
    neg_size = lax.axis_size("neg")
    devices = dp_size * neg_size
    capacity = max(2, 2 * list_len // devices)
    slot_count = devices * capacity
    entry = jnp.arange(list_len, dtype=jnp.int32)
    same_owner = owners[:, None] == owners[None, :]
    earlier = entry[:, None] > entry[None, :]
    slot_rank = jnp.sum((same_owner & earlier).astype(jnp.int32), axis=1)
    slot_index = owners * capacity + slot_rank
    place_table = jnp.arange(slot_count, dtype=jnp.int32)[:, None] == slot_index[None, :]
    place_bf = place_table.astype(jnp.bfloat16)
    requests = jnp.sum(jnp.where(place_table, row_ids[None, :] + 1, 0), axis=1)
    asked_rows = lax.all_to_all(
        requests.reshape(devices, capacity), ("dp", "neg"), split_axis=0, concat_axis=0, tiled=True
    )
    asked_rows = asked_rows.reshape(-1)
    pass_rows = passages.shape[0]
    pick_table = (
        asked_rows[:, None] - 1 == jnp.arange(pass_rows, dtype=jnp.int32)[None, :]
    ).astype(jnp.bfloat16)
    outgoing = jnp.dot(pick_table, passages, preferred_element_type=jnp.float32).astype(
        jnp.bfloat16
    )
    incoming = lax.all_to_all(
        outgoing.reshape(devices, capacity, width),
        ("dp", "neg"),
        split_axis=0,
        concat_axis=0,
        tiled=True,
    )
    incoming = incoming.reshape(slot_count, width)
    own_rows = lax.dot_general(
        place_bf, incoming, (((0,), (0,)), ((), ())), preferred_element_type=jnp.float32
    ).astype(jnp.bfloat16)
    column_block = lax.all_gather(own_rows, "dp", axis=0, tiled=True)
    block_rows = column_block.shape[0]
    logit_scale = 3.0 / math.sqrt(width)
    logits = (
        lax.dot_general(
            queries, column_block, (((1,), (1,)), ((), ())), preferred_element_type=jnp.float32
        )
        * logit_scale
    )
    local_max = jnp.max(logits, axis=1)
    local_sum = jnp.sum(jnp.exp(logits - local_max[:, None]), axis=1)
    row_max = lax.pmax(local_max, "neg")
    row_total = lax.psum(local_sum * jnp.exp(local_max - row_max), "neg")
    probability = jnp.exp(logits - row_max[:, None]) / row_total[:, None]
    first_col = lax.axis_index("neg") * block_rows
    target = (
        positive[:, None] == first_col + jnp.arange(block_rows, dtype=jnp.int32)[None, :]
    ).astype(jnp.float32)
    logit_grad = (row_weight[:, None] * logit_scale * (probability - target)).astype(jnp.bfloat16)
    partial_value = jnp.dot(logit_grad, column_block, preferred_element_type=jnp.float32)
    query_grad = lax.psum_scatter(
        partial_value.astype(jnp.bfloat16), "neg", scatter_dimension=1, tiled=True
    )
    column_grad = lax.psum_scatter(
        lax.dot_general(
            logit_grad, queries, (((0,), (0,)), ((), ())), preferred_element_type=jnp.float32
        ).astype(jnp.bfloat16),
        "dp",
        scatter_dimension=0,
        tiled=True,
    ).astype(jnp.float32)
    slot_entry = jnp.sum(jnp.where(place_table, entry[None, :] + 1, 0), axis=1) - 1
    send_slots = jnp.where((slot_entry >= 0)[:, None], column_grad[jnp.maximum(slot_entry, 0)], 0.0)
    returned = lax.all_to_all(
        send_slots.reshape(devices, capacity, width).astype(jnp.bfloat16),
        ("dp", "neg"),
        split_axis=0,
        concat_axis=0,
        tiled=True,
    ).astype(jnp.float32)
    returned = returned.reshape(slot_count, width)
    passage_grad = lax.dot_general(
        pick_table.astype(jnp.float32),
        returned,
        (((0,), (0,)), ((), ())),
        precision=lax.Precision.HIGHEST,
        preferred_element_type=jnp.float32,
    )
    return (query_grad, passage_grad)


def solution(mesh):
    in_specs = (
        P("dp", None),
        P(("dp", "neg"), None),
        P("neg", "dp", None),
        P("neg", "dp"),
        P("dp"),
        P("dp"),
    )
    out_specs = (P("dp", "neg"), P(("dp", "neg"), None))
    return jax.shard_map(body, mesh=mesh, in_specs=in_specs, out_specs=out_specs, check_vma=False)
```

profile of v0, /device:TPU:0, one launch (start us, length us, event | category | flops | bytes accessed | tf_op | source)
XLA Modules:
  0.0 366.7 jit_solution(12786644786598306239)
XLA Ops:
  7.2 0.0 copy-start
  7.2 0.0 all-gather.2.cloned.1.call-start
  7.2 1.0 convert_reduce_fusion
  8.2 0.7 iota_add_fusion.1
  8.9 0.7 add_bitcast_fusion
  9.5 0.1 select_reduce_fusion
  9.7 0.1 all_to_all.12
  9.8 14.3 %all_to_all.19 = s32[32,1,8]{2,1,0:T(1,128)S(1)} all-to-all(s32[32,1,8]{2,1,0:T(1,128)S(1)} %bitcast.30), channel_id=1, replica_groups=mesh['dp'=8,'neg'=4] {'dp','neg'}, dimensions={0} | all-to-all | bytes 2048 | tf_op jit(solution)/shard_map/all_to_all | solution.py:27
  24.1 0.1 sub.35
  24.2 0.0 copy-done
  24.2 0.8 fusion
  24.9 49.3 %all_to_all.20 = bf16[32,8,4096]{2,1,0:T(8,128)(2,1)S(1)} all-to-all(bf16[32,8,4096]{2,1,0:T(8,128)(2,1)S(1)} %fusion), channel_id=1, replica_groups=mesh['dp'=8,'neg'=4] {'dp','neg'}, dimensions={0} | all-to-all | bytes 4194304 | tf_op jit(solution)/shard_map/all_to_all | solution.py:38
  74.2 1.5 convolution_convert_fusion.3
  75.7 0.0 all-gather.2.cloned.1.call-update
  75.7 0.0 reduce-scatter.5.cloned.1.call-start
  75.7 0.0 copy-done.1
  75.8 54.3 %all-gather.2.cloned.1.call-done = bf16[1024,4096]{1,0:T(8,128)(2,1)} async-done(((bf16[128,4096]{1,0:T(8,128)(2,1)}), bf16[1024,4096]{1,0:T(8,128)(2,1)}) %all-gather.2.cloned.1.call-update) | async-done | bytes 8388624 | tf_op jit(solution)/shard_map/all_gather | solution.py:49
  130.0 10.4 %multiply_reduce_fusion = (f32[512]{0:T(512)S(1)}, f32[1024,512]{1,0:T(8,128)}) fusion(bf16[1024,4096]{1,0:T(8,128)(2,1)} %all-gather.2.cloned.1.call-done, bf16[512,4096]{1,0:T(8,128)(2,1)} %param.6), kind=kOutput, calls=%fused_computation.15 | convolution fusion | flops 4296015360 | bytes 14682112 | tf_op jit(solution)/shard_map/dot_general | solution.py:53
  140.4 11.8 %pmax.7 = f32[512]{0:T(512)S(1)} all-reduce(f32[512]{0:T(512)S(1)} %get-tuple-element.4), channel_id=1, replica_groups=mesh['dp'=8,'neg'=4] {'neg'}, use_global_device_ids=true, to_apply=%region_3.4 | all-reduce | flops 512 | bytes 4096 | tf_op jit(solution)/shard_map/pmax | solution.py:60
  152.2 2.0 exponential_reduce_fusion
  154.2 8.4 %psum.7 = f32[512]{0:T(512)S(1)} all-reduce(f32[512]{0:T(512)S(1)} %exponential_multiply_fusion), channel_id=1, replica_groups=mesh['dp'=8,'neg'=4] {'neg'}, use_global_device_ids=true, to_apply=%region_5.6 | all-reduce | flops 512 | bytes 4096 | tf_op jit(solution)/shard_map/psum | solution.py:61
  162.6 10.8 %convolution_convert_fusion = bf16[1024,4096]{1,0:T(8,128)(2,1)} fusion(bf16[512,4096]{1,0:T(8,128)(2,1)} %param.6, f32[1024,512]{1,0:T(8,128)} %get-tuple-element.5, s32[512]{0:T(512)S(1)} %copy-done.2, f32[512]{0:T(512)S(1)} %psum.7, f32[512]{0:T(512)S(1)} %pmax.7, f32[512]{0:T(512)S(1)} %broadcast_multiply_fusion, s32[1024]{0:T(1024)S(1)} %iota_add_fusion), kind=kOutput, calls=%fused_computation.1 | convolution fusion | flops 4303355904 | bytes 14692352 | tf_op jit(solution)/shard_map/dot_general | solution.py:73
  173.5 0.0 reduce-scatter.5.cloned.1.call-update
  173.5 0.2 reduce-scatter.3.cloned.1.call-start
  173.7 11.2 %convolution_convert_fusion.1 = bf16[512,4096]{1,0:T(8,128)(2,1)} fusion(bf16[1024,4096]{1,0:T(8,128)(2,1)} %all-gather.2.cloned.1.call-done, f32[1024,512]{1,0:T(8,128)} %get-tuple-element.5, s32[512]{0:T(512)S(1)} %copy-done.2, f32[512]{0:T(512)S(1)} %psum.7, f32[512]{0:T(512)S(1)} %pmax.7, f32[512]{0:T(512)S(1)} %broadcast_multiply_fusion, ...), kind=kOutput, calls=%fused_computation.2 | convolution fusion | flops 4301258752 | bytes 14692352 | tf_op jit(solution)/shard_map/dot_general | solution.py:68
  185.0 0.0 reduce-scatter.3.cloned.1.call-update
  185.0 0.1 ge.11
  185.1 58.5 %reduce-scatter.5.cloned.1.call-done = bf16[128,4096]{1,0:T(8,128)(2,1)} async-done(((bf16[1024,4096]{1,0:T(8,128)(2,1)}), bf16[128,4096]{1,0:T(8,128)(2,1)}) %reduce-scatter.5.cloned.1.call-update) | async-done | bytes 1048592 | tf_op jit(solution)/shard_map/reduce_scatter | solution.py:72
  243.6 6.6 %gather_fusion = bf16[256,4096]{1,0:T(8,128)(2,1)} fusion(bf16[128,4096]{1,0:T(8,128)(2,1)} %reduce-scatter.5.cloned.1.call-done, s32[1024]{0:T(1024)S(1)} %pad_clamp_fusion), kind=kCustom, calls=%fused_computation | custom fusion | bytes 4195328 | tf_op jit(solution)/shard_map/gather | solution.py:81
  250.2 2.2 fusion.1
  252.3 105.0 %all_to_all.21 = bf16[32,8,4096]{2,1,0:T(8,128)(2,1)S(1)} all-to-all(bf16[32,8,4096]{2,1,0:T(8,128)(2,1)S(1)} %fusion.1), channel_id=1, replica_groups=mesh['dp'=8,'neg'=4] {'dp','neg'}, dimensions={0} | all-to-all | bytes 4194304 | tf_op jit(solution)/shard_map/all_to_all | solution.py:82
  357.3 2.8 fusion.2
  (11 shorter events, 0.1 us)
Async XLA Ops:
  7.2 17.0 %copy-start = (bf16[256,4096]{1,0:T(8,128)(2,1)S(1)}, bf16[256,4096]{1,0:T(8,128)(2,1)}, u32[]{:S(2)}) copy-start(bf16[256,4096]{1,0:T(8,128)(2,1)} %param.7) | copy-start | bytes 6291460
  7.2 122.8 %all-gather.2.cloned.1.call-start = ((), (), s32[]{:S(2)}) async-start(), calls=%async_computation.5 | async-start | bytes 9437184 | tf_op jit(solution)/shard_map/all_gather | solution.py:49
  74.2 1.6 copy-start.1
  75.7 167.9 %reduce-scatter.5.cloned.1.call-start = ((), (), s32[]{:S(2)}) async-start(), calls=%async_computation.7 | async-start | bytes 9437184 | tf_op jit(solution)/shard_map/reduce_scatter | solution.py:72
  140.4 22.2 %copy-start.2 = (s32[512]{0:T(512)S(1)}, s32[512]{0:T(512)}, u32[]{:S(2)}) copy-start(s32[512]{0:T(512)} %param.10) | copy-start | bytes 6148
  173.5 186.6 %reduce-scatter.3.cloned.1.call-start = ((), (), s32[]{:S(2)}) async-start(), calls=%async_computation.6 | async-start | bytes 5242880 | tf_op jit(solution)/shard_map/reduce_scatter | solution.py:69
Sparse Core Ops, SparseCore 0:
  75.8 54.1 all-gather.1
  173.6 69.9 reduce-scatter.4
  246.6 113.3 reduce-scatter.2
where the time goes:
time: 374 us; the launch traced here: 367 us
  blocking collectives  189 us (51%)
  waiting for transfers between devices  113 us (30%)
  matrix products  37.5 us (10%)
  between operations  13.8 us (4%)
  local copies, waits for them, and re-layouts  6.84 us (2%)
  other arithmetic  6.69 us (2%)
    all_to_all x1, blocking collectives, body(): lax.all_to_all(send_slots.reshape(devices, capacity, width).astype(jnp.bf...  105 us
    reduce_scatter x1, waiting for transfers between devices, body(): lax.psum_scatter(lax.dot_general(logit_grad, queries, (((0,), (0,)), ((),...  58.5 us
    all_gather x1, waiting for transfers between devices, body(): column_block = lax.all_gather(own_rows, 'dp', axis=0, tiled=True)  54.3 us
    all_to_all x1, blocking collectives, body(): lax.all_to_all(outgoing.reshape(devices, capacity, width), ('dp', 'neg'),...  49.3 us
    all_to_all x1, blocking collectives, body(): lax.all_to_all(requests.reshape(devices, capacity), ('dp', 'neg'), split_...  14.3 us
    pmax x1, blocking collectives, body(): row_max = lax.pmax(local_max, 'neg')  11.8 us
    dot_general x1, matrix products, body(): jnp.dot(logit_grad, column_block, preferred_element_type=jnp.float32)  11.2 us
    dot_general x1, matrix products, body(): lax.dot_general(logit_grad, queries, (((0,), (0,)), ((), ())), preferred_...  10.8 us
  transfers between devices with their start and end apart: 3, of which 2 were waited for; matrix products, arithmetic and copies ran while one was open for 6% of the time, Pallas kernels for 0%

commit v1 on v0

v1 whole, which is shorter than its diff:
```python
import math

import jax
import jax.numpy as jnp
from jax import lax
from jax.sharding import PartitionSpec as P

F32 = jnp.float32
BF16 = jnp.bfloat16


def one_hot(index, size):
    return (index[:, None] == jnp.arange(size, dtype=jnp.int32)[None, :]).astype(BF16)


def dot_f32(a, b, dims):
    return lax.dot_general(a, b, (dims, ((), ())), preferred_element_type=F32)


def once(ready, value):
    corner = ready[(0,) * ready.ndim]
    return jnp.where(corner == corner, value, jnp.zeros_like(value))


def add_bf16(a, b):
    return (a.astype(F32) + b.astype(F32)).astype(BF16)


def shift_gather(value, axis, size):
    got = [value]
    for hop in range(1, size):
        got.append(lax.ppermute(value, axis, [(j, (j + hop) % size) for j in range(size)]))
    return got


def exchange(parts, axis):
    return lax.all_to_all(parts, axis, split_axis=0, concat_axis=0, tiled=True)


def swap(value, bit):
    return lax.ppermute(value, "dp", [(d, d ^ bit) for d in range(8)])


def rank_rows(counts):
    order = jnp.arange(counts.shape[1], dtype=jnp.int32)
    upto = (order[:, None] <= order[None, :]).astype(BF16)
    ends = dot_f32((counts > 0).astype(BF16), upto, ((1,), (0,))).astype(jnp.int32)
    return ends - 1, jnp.max(ends)


def pick_rows(room, counts, rank, mine):
    own_counts = lax.dynamic_index_in_dim(counts, mine, axis=0, keepdims=False)
    own_rank = lax.dynamic_index_in_dim(rank, mine, axis=0, keepdims=False)
    slots = jnp.arange(room, dtype=jnp.int32)
    return ((own_rank[None, :] == slots[:, None]) & (own_counts[None, :] > 0)).astype(BF16)


def lift_of(times):
    return jnp.where(times > 0, jnp.log(jnp.maximum(times, 1.0)), -1e30)


def describe_slots(room, counts, rank, first_id):
    slots = jnp.arange(room, dtype=jnp.int32)
    order = jnp.arange(counts.shape[1], dtype=jnp.int32)
    chosen = (rank[:, None, :] == slots[None, :, None]) & (counts[:, None, :] > 0)
    times = jnp.sum(jnp.where(chosen, counts[:, None, :], 0.0), axis=2)
    names = first_id[:, None] + order[None, :] + 1
    column_id = jnp.sum(jnp.where(chosen, names[:, None, :], 0), axis=2) - 1
    return lift_of(times), column_id


def logits_of(queries, columns, lift):
    scale = 3.0 / math.sqrt(queries.shape[1])
    return dot_f32(columns, queries, ((1,), (1,))) * scale + lift[:, None]


def softmax_grads(logits, column_ids, pos_id, row_weight, width, n_neg):
    factor = row_weight * (3.0 / math.sqrt(width))
    local_max = jnp.max(logits[0], axis=0)
    for group in logits[1:]:
        local_max = jnp.maximum(local_max, jnp.max(group, axis=0))
    expos = [jnp.exp(group - local_max[None, :]) for group in logits]
    local_sum = sum(jnp.sum(group, axis=0) for group in expos)
    stats = shift_gather(jnp.stack([local_max, local_sum]), "neg", n_neg)
    row_max = stats[0][0]
    for other in stats[1:]:
        row_max = jnp.maximum(row_max, other[0])
    row_total = sum(other[1] * jnp.exp(other[0] - row_max) for other in stats)
    share = factor * jnp.exp(local_max - row_max) / row_total
    return [
        (
            expo * share[None, :]
            - jnp.where(column_id[:, None] == pos_id[None, :], factor[None, :], 0.0)
        ).astype(BF16)
        for expo, column_id in zip(expos, column_ids)
    ]


def gather_cube(rows):
    half = rows.shape[0] // 2
    over_x = swap(rows, 2)
    over_y = swap(rows, 4)
    far = [swap(over_x[:half], 4), swap(over_y[half:], 2)]
    return rows, over_x, over_y, far


def scatter_cube(total):
    room = total.shape[0] // 4
    half = room // 2
    mine, to_x, to_y, far = [total[t * room:(t + 1) * room] for t in range(4)]
    far_first = swap(far[:half], 4)
    far_last = swap(far[half:], 2)
    x_last = swap(to_x[half:], 2)
    y_first = swap(to_y[:half], 4)
    x_first = swap(add_bf16(to_x[:half], far_first), 2)
    y_last = swap(add_bf16(to_y[half:], far_last), 4)
    from_x = jnp.concatenate([x_first, x_last])
    from_y = jnp.concatenate([y_first, y_last])
    return (mine.astype(F32) + from_x.astype(F32) + from_y.astype(F32)).astype(BF16)


def gradients_cube(room, queries, passages, counts, pos_id, row_weight, n_neg):
    pass_rows, width = passages.shape
    i_dp = lax.axis_index("dp")
    i_neg = lax.axis_index("neg")
    rank, _ = rank_rows(counts)
    pick = pick_rows(room, counts, rank, i_dp * n_neg + i_neg)
    rows = dot_f32(pick, passages, ((1,), (0,))).astype(BF16)
    rows = lax.optimization_barrier(rows)
    rows, over_x, over_y, far = gather_cube(rows)
    over_core = swap(rows, 1)

    turn = jnp.arange(8, dtype=jnp.int32)
    owners = (i_dp ^ (turn % 4 * 2 + turn // 4)) * n_neg + i_neg
    lift, slot_id = describe_slots(room, counts[owners], rank[owners], owners * pass_rows)

    groups, logits, column_ids = [], [], []

    def take(blocks, first, stop, step):
        groups.append(jnp.concatenate(blocks))
        logits.append(logits_of(queries, groups[-1], lift[first:stop:step].reshape(-1)))
        column_ids.append(slot_id[first:stop:step].reshape(-1))

    take([rows, over_core], 0, 5, 4)
    take([over_x, over_y], 1, 3, 1)
    take([swap(over_x, 1), swap(over_y, 1)], 5, 7, 1)
    far = once(logits[-1], jnp.concatenate(far))
    take([far, swap(far, 1)], 3, 8, 4)
    columns = jnp.concatenate(groups)
    grads = softmax_grads(logits, column_ids, pos_id, row_weight, width, n_neg)
    logit_grad = lax.optimization_barrier(jnp.concatenate(grads))
    query_part = dot_f32(logit_grad, columns, ((0,), (0,))).astype(BF16)
    query_grad = lax.psum_scatter(query_part, "neg", scatter_dimension=1, tiled=True)

    def grad_rows(*places):
        return jnp.concatenate([logit_grad[begin * room:stop * room] for begin, stop in places])

    across = dot_f32(grad_rows((1, 2), (4, 6), (7, 8)), queries, ((1,), (0,))).astype(BF16)
    near = dot_f32(grad_rows((0, 1), (2, 4), (6, 7)), queries, ((1,), (0,))).astype(BF16)
    column_grad = scatter_cube(add_bf16(near, swap(across, 1)))
    return query_grad, dot_f32(pick, column_grad, ((0,), (0,)))


def gradients_plain(room, queries, passages, counts, pos_id, row_weight, n_dp, n_neg):
    pass_rows, width = passages.shape
    rank, _ = rank_rows(counts)
    i_dp = lax.axis_index("dp")
    i_neg = lax.axis_index("neg")
    pick = pick_rows(room, counts, rank, i_dp * n_neg + i_neg)
    rows = dot_f32(pick, passages, ((1,), (0,))).astype(BF16)
    columns = exchange(jnp.broadcast_to(rows, (n_dp, room, width)), "dp")
    columns = columns.reshape(n_dp * room, width)
    owners = jnp.arange(n_dp, dtype=jnp.int32) * n_neg + i_neg
    lift, column_id = describe_slots(room, counts[owners], rank[owners], owners * pass_rows)
    logits = logits_of(queries, columns, lift.reshape(-1))
    (logit_grad,) = softmax_grads(
        [logits], [column_id.reshape(-1)], pos_id, row_weight, width, n_neg
    )
    query_part = dot_f32(logit_grad, columns, ((0,), (0,))).astype(BF16)
    query_part = query_part.reshape(query_part.shape[0], n_neg, -1).swapaxes(0, 1)
    query_grad = jnp.sum(exchange(query_part, "neg").astype(F32), axis=0).astype(BF16)
    column_part = dot_f32(logit_grad, queries, ((1,), (0,))).astype(BF16)
    column_part = column_part.reshape(n_dp, room, width)
    column_grad = jnp.sum(exchange(column_part, "dp").astype(F32), axis=0).astype(BF16)
    return query_grad, dot_f32(pick, column_grad, ((0,), (0,)))


def body(n_dp, n_neg, queries, passages, list_owner, list_row, positive, row_weight):
    devices = n_dp * n_neg
    pass_rows = passages.shape[0]
    list_len = list_row.shape[1]
    packed = list_owner.reshape(-1) * pass_rows + list_row.reshape(-1)
    ids = lax.all_to_all(
        jnp.broadcast_to(packed, (devices, list_len)),
        ("neg", "dp"),
        split_axis=0,
        concat_axis=0,
        tiled=True,
    ).reshape(-1)
    owner_of = ids // pass_rows
    row_of = ids % pass_rows
    counts = dot_f32(one_hot(owner_of, devices), one_hot(row_of, pass_rows), ((0,), (0,)))
    high = one_hot(positive // list_len, devices)
    low = one_hot(positive % list_len, list_len).astype(F32)
    owner_table = owner_of.reshape(-1, list_len).astype(BF16)
    row_table = row_of.reshape(-1, list_len).astype(BF16)
    pos_owner = jnp.sum(dot_f32(high, owner_table, ((1,), (0,))) * low, axis=1)
    pos_row = jnp.sum(dot_f32(high, row_table, ((1,), (0,))) * low, axis=1)
    pos_id = pos_owner.astype(jnp.int32) * pass_rows + pos_row.astype(jnp.int32)

    def plain(room):
        return gradients_plain(
            room, queries, passages, counts, pos_id, row_weight, n_dp, n_neg
        )

    _, longest = rank_rows(counts)
    if n_dp == 8:
        grads = gradients_cube(list_len, queries, passages, counts, pos_id, row_weight, n_neg)
    else:
        grads = plain(list_len)
    _, query_grad, passage_grad = lax.while_loop(
        lambda state: state[0],
        lambda state: (jnp.zeros((), jnp.bool_), *plain(pass_rows)),
        (longest > list_len, *grads),
    )
    return query_grad, passage_grad


def solution(mesh):
    n_dp, n_neg = mesh.shape["dp"], mesh.shape["neg"]
    in_specs = (
        P("dp", None),
        P(("dp", "neg"), None),
        P("neg", "dp", None),
        P("neg", "dp"),
        P("dp"),
        P("dp"),
    )
    out_specs = (P("dp", "neg"), P(("dp", "neg"), None))

    def run(*args):
        return body(n_dp, n_neg, *args)

    return jax.shard_map(run, mesh=mesh, in_specs=in_specs, out_specs=out_specs, check_vma=False)
```

time: 374 us -> 169 us (0.45); the launches traced: 367 us -> 168 us
  blocking collectives: 189 us -> 0 us
  starting transfers between devices: 0.3 us -> 19.4 us
  waiting for transfers between devices: 113 us -> 95.3 us
  matrix products: 37.5 us -> 28.3 us
    all_to_all x3 -> x0, blocking collectives: 168 us -> none  [the longest x1 105 us: body(): lax.all_to_all(send_slots.reshape(devices, capacity, width).astype(jnp.bf...]
    ppermute x0 -> x18, waiting for transfers between devices: none -> 71.1 us  [the longest x15 66.4 us: swap(): return lax.ppermute(value, 'dp', [(d, d ^ bit) for d in range(8)])]
    all_gather x1 -> x0, waiting for transfers between devices: 54.3 us -> none  [body(): column_block = lax.all_gather(own_rows, 'dp', axis=0, tiled=True)]
    reduce_scatter x2 -> x1, waiting for transfers between devices: 58.5 us -> 17.1 us  [gradients_cube(): lax.psum_scatter(query_part, 'neg', scatter_dimension=1, tiled=True)]
    ppermute x0 -> x18, starting transfers between devices: none -> 12.1 us  [the longest x15 9.4 us: swap(): return lax.ppermute(value, 'dp', [(d, d ^ bit) for d in range(8)])]
    pmax x1 -> x0, blocking collectives: 11.8 us -> none  [body(): row_max = lax.pmax(local_max, 'neg')]
    dot_general x6 -> x13, matrix products: 37.5 us -> 28.3 us  [dot_f32(): return lax.dot_general(a, b, (dims, ((), ())), preferred_element_type=F32)]
    psum x1 -> x0, blocking collectives: 8.41 us -> none  [body(): row_total = lax.psum(local_sum * jnp.exp(local_max - row_max), 'neg')]
  transfers between devices with their start and end apart: 3 -> 20, of which waited for: 2 -> 14; matrix products, arithmetic and copies ran while one was open for 6% -> 13% of each run, Pallas kernels for 0% -> 0%
where the time goes in v1:
time: 169 us; the launch traced here: 168 us
  waiting for transfers between devices  95.3 us (56%)
  matrix products  28.3 us (17%)
  starting transfers between devices  19.4 us (11%)
  between operations  16.4 us (10%)
  local copies, waits for them, and re-layouts  5.59 us (3%)
  other arithmetic  3.47 us (2%)
    ppermute x15, waiting for transfers between devices, swap(): return lax.ppermute(value, 'dp', [(d, d ^ bit) for d in range(8)])  66.4 us
    dot_general x13, matrix products, dot_f32(): return lax.dot_general(a, b, (dims, ((), ())), preferred_element_type=F32)  28.3 us
    reduce_scatter x1, waiting for transfers between devices, gradients_cube(): lax.psum_scatter(query_part, 'neg', scatter_dimension=1, tiled=True)  17.1 us
    ppermute x15, starting transfers between devices, swap(): return lax.ppermute(value, 'dp', [(d, d ^ bit) for d in range(8)])  9.4 us
    all_to_all x1, starting transfers between devices, body(): lax.all_to_all(jnp.broadcast_to(packed, (devices, list_len)), ('neg', 'dp...  7.3 us
    all_to_all x1, waiting for transfers between devices, body(): lax.all_to_all(jnp.broadcast_to(packed, (devices, list_len)), ('neg', 'dp...  7 us
    ppermute x3, waiting for transfers between devices, shift_gather(): lax.ppermute(value, axis, [(j, (j + hop) % size) for j in range(size)])  4.74 us
  transfers between devices with their start and end apart: 20, of which 14 were waited for; matrix products, arithmetic and copies ran while one was open for 13% of the time, Pallas kernels for 0%

profile of v1, /device:TPU:0, one launch (start us, length us, event | category | flops | bytes accessed | tf_op | source)
XLA Modules:
  0.0 168.4 jit_solution(17128310180097637574)
XLA Ops:
  9.3 7.3 %all-to-all-start.3 = ((s32[32,1,128]{2,1,0:T(1,128)}), s32[32,1,128]{2,1,0:T(1,128)S(1)}, u32[]{:S(2)}, u32[]{:S(2)}) async-start(s32[32,1,128]{2,1,0:T(1,128)} %broadcast_in_dim.89), calls=%async_computation.3 | async-start | bytes 32768 | tf_op jit(solution)/shard_map/all_to_all | solution.py:193
  16.6 7.0 %all-to-all-done.3 = s32[32,1,128]{2,1,0:T(1,128)S(1)} async-done(((s32[32,1,128]{2,1,0:T(1,128)}), s32[32,1,128]{2,1,0:T(1,128)S(1)}, u32[]{:S(2)}, u32[]{:S(2)}) %all-to-all-start.3) | async-done | bytes 16416 | tf_op jit(solution)/shard_map/all_to_all | solution.py:193
  23.7 0.9 fusion.20
  24.6 0.8 broadcast_add_fusion
  26.6 2.0 %convolution_convert_fusion.7 = bf16[128,4096]{1,0:T(8,128)(2,1)S(1)} fusion(bf16[256,4096]{1,0:T(8,128)(2,1)} %param.9, s32[256]{0:T(256)S(1)} %bitcast.90, pred[256]{0:T(512)(128)(4,1)S(1)} %compare_reduce_fusion.1), kind=kOutput, calls=%fused_computation.53 | convolution fusion | flops 269025280 | bytes 3147008 | tf_op jit(solution)/shard_map/dot_general | solution.py:17
  31.3 22.3 %collective-permute-done.5 = bf16[128,4096]{1,0:T(8,128)(2,1)S(1)} collective-permute-done((bf16[128,4096]{1,0:T(8,128)(2,1)S(1)}, bf16[128,4096]{1,0:T(8,128)(2,1)S(1)}, u32[]{:S(2)}, u32[]{:S(2)}) %collective-permute-start.5) | collective-permute-done | bytes 1048608 | tf_op jit(solution)/shard_map/ppermute | solution.py:41
  54.3 1.2 collective-permute-start.8
  56.0 1.3 constant_dynamic-update-slice_fusion.6
  57.5 2.2 %collective-permute-done.6 = bf16[128,4096]{1,0:T(8,128)(2,1)S(1)} collective-permute-done((bf16[128,4096]{1,0:T(8,128)(2,1)S(1)}, bf16[128,4096]{1,0:T(8,128)(2,1)S(1)}, u32[]{:S(2)}, u32[]{:S(2)}) %collective-permute-start.6) | collective-permute-done | bytes 1048608 | tf_op jit(solution)/shard_map/ppermute | solution.py:41
  59.8 1.3 fusion.144
  63.0 3.6 %collective-permute-done.9 = bf16[64,4096]{1,0:T(8,128)(2,1)S(1)} collective-permute-done((bf16[64,4096]{1,0:T(8,128)(2,1)S(1)}, bf16[64,4096]{1,0:T(8,128)(2,1)S(1)}, u32[]{:S(2)}, u32[]{:S(2)}) %collective-permute-start.9) | collective-permute-done | bytes 524320 | tf_op jit(solution)/shard_map/ppermute | solution.py:41
  67.2 1.3 fusion.146
  68.6 2.5 %fusion.145 = (f32[512]{0:T(512)S(1)}, f32[256,512]{1,0:T(8,128)S(1)}) fusion(f32[256]{0:T(256)S(1)} %bitcast.101, bf16[512,4096]{1,0:T(8,128)(2,1)S(1)} %copy-done.6, bf16[128,4096]{1,0:T(8,128)(2,1)} %collective-permute-done.3, bf16[128,4096]{1,0:T(8,128)(2,1)S(1)} %convolution_convert_fusion.7), kind=kOutput, calls=%fused_computation.241 | convolution fusion | flops 1078328832 | bytes 6818816 | tf_op jit(solution)/shard_map/dot_general | solution.py:17
  71.1 1.3 fusion.143
  73.4 1.5 collective-permute-start.12
  75.6 0.9 collective-permute-done.13
  76.5 1.4 collective-permute-done.12
  77.9 2.4 %collective-permute-done.11 = f32[2,512]{1,0:T(2,128)S(1)} collective-permute-done((f32[2,512]{1,0:T(2,128)S(1)}, f32[2,512]{1,0:T(2,128)S(1)}, u32[]{:S(2)}, u32[]{:S(2)}) %collective-permute-start.11) | collective-permute-done | bytes 4128 | tf_op jit(solution)/shard_map/ppermute | solution.py:32
  81.1 6.3 %convolution_convert_fusion.4 = bf16[512,4096]{1,0:T(8,128)(2,1)} fusion(bf16[1024,512]{1,0:T(8,128)(2,1)S(1)} %pad_maximum_fusion.1, bf16[1024,4096]{1,0:T(8,128)(2,1)S(1)} %constant_dynamic-update-slice_fusion), kind=kOutput, calls=%fused_computation.50 | convolution fusion | flops 4297064448 | bytes 13631488 | tf_op jit(solution)/shard_map/dot_general | solution.py:17
  87.4 4.7 %convolution_convert_fusion.5 = bf16[512,4096]{1,0:T(8,128)(2,1)S(1)} fusion(bf16[512,4096]{1,0:T(8,128)(2,1)} %param.8, bf16[128,512]{1,0:T(8,128)(2,1)S(1)} %get-tuple-element.75, bf16[256,512]{1,0:T(8,128)(2,1)S(1)} %get-tuple-element.79, bf16[128,512]{1,0:T(8,128)(2,1)S(1)} %get-tuple-element.76), kind=kOutput, calls=%fused_computation.51 | convolution fusion | flops 2151153664 | bytes 8912896 | tf_op jit(solution)/shard_map/dot_general | solution.py:17
  92.2 7.1 %collective-permute-done.14 = bf16[512,4096]{1,0:T(8,128)(2,1)S(1)} collective-permute-done((bf16[512,4096]{1,0:T(8,128)(2,1)S(1)}, bf16[512,4096]{1,0:T(8,128)(2,1)S(1)}, u32[]{:S(2)}, u32[]{:S(2)}) %collective-permute-start.14) | collective-permute-done | bytes 4194336 | tf_op jit(solution)/shard_map/ppermute | solution.py:41
  99.3 2.3 %add_convert_fusion = bf16[512,4096]{1,0:T(8,128)(2,1)S(1)} fusion(bf16[512,4096]{1,0:T(8,128)(2,1)S(1)} %collective-permute-done.14, bf16[512,4096]{1,0:T(8,128)(2,1)S(1)} %copy-done.7, bf16[128,512]{1,0:T(8,128)(2,1)S(1)} %get-tuple-element.77, bf16[256,512]{1,0:T(8,128)(2,1)S(1)} %get-tuple-element.78, bf16[128,512]{1,0:T(8,128)(2,1)S(1)} %get-tuple-element.74), kind=kOutput, calls=%fused_computation.49 | convolution fusion | flops 2159542272 | bytes 13107200 | tf_op jit(solution)/shard_map/dot_general | solution.py:17
  101.7 1.3 fusion.137
  103.0 1.2 collective-permute-start.19
  105.0 1.3 collective-permute-start.18
  107.1 10.7 %collective-permute-done.19 = bf16[64,4096]{1,0:T(8,128)(2,1)S(1)} collective-permute-done((bf16[64,4096]{1,0:T(8,128)(2,1)S(1)}, bf16[64,4096]{1,0:T(8,128)(2,1)S(1)}, u32[]{:S(2)}, u32[]{:S(2)}) %collective-permute-start.19) | collective-permute-done | bytes 524320 | tf_op jit(solution)/shard_map/ppermute | solution.py:41
  117.8 1.3 collective-permute-done.15
  120.1 0.9 collective-permute-start.16
  121.6 8.7 %collective-permute-done.18 = bf16[64,4096]{1,0:T(8,128)(2,1)S(1)} collective-permute-done((bf16[64,4096]{1,0:T(8,128)(2,1)}, bf16[64,4096]{1,0:T(8,128)(2,1)S(1)}, u32[]{:S(2)}, u32[]{:S(2)}) %collective-permute-start.18) | collective-permute-done | bytes 524320 | tf_op jit(solution)/shard_map/ppermute | solution.py:41
  130.3 10.1 %collective-permute-done.20 = bf16[64,4096]{1,0:T(8,128)(2,1)S(1)} collective-permute-done((bf16[64,4096]{1,0:T(8,128)(2,1)S(1)}, bf16[64,4096]{1,0:T(8,128)(2,1)S(1)}, u32[]{:S(2)}, u32[]{:S(2)}) %collective-permute-start.20) | collective-permute-done | bytes 524320 | tf_op jit(solution)/shard_map/ppermute | solution.py:41
  140.4 4.0 %fusion.64 = f32[256,4096]{1,0:T(8,128)} fusion(bf16[512,4096]{1,0:T(8,128)(2,1)} %copy-done.1, bf16[64,4096]{1,0:T(8,128)(2,1)S(1)} %collective-permute-done.17, bf16[64,4096]{1,0:T(8,128)(2,1)S(1)} %collective-permute-done.16, bf16[64,4096]{1,0:T(8,128)(2,1)S(1)} %collective-permute-done.20, bf16[64,4096]{1,0:T(8,128)(2,1)S(1)} %collective-permute-done.18, ...), kind=kOutput, calls=%fused_computation.87 | convolution fusion | flops 274792448 | bytes 7341312 | tf_op jit(solution)/shard_map/dot_general | solution.py:17
  144.4 17.1 %reduce-scatter.2.cloned.1.call-done = bf16[512,1024]{1,0:T(8,128)(2,1)} async-done(((bf16[512,4096]{1,0:T(8,128)(2,1)}), bf16[512,1024]{1,0:T(8,128)(2,1)}) %reduce-scatter.2.cloned.1.call-update) | async-done | bytes 1048592 | tf_op jit(solution)/shard_map/reduce_scatter | solution.py:153
  (86 shorter events, 13.5 us)
Async XLA Ops:
  9.3 14.4 %all-to-all-start.3 = ((s32[32,1,128]{2,1,0:T(1,128)}), s32[32,1,128]{2,1,0:T(1,128)S(1)}, u32[]{:S(2)}, u32[]{:S(2)}) async-start(s32[32,1,128]{2,1,0:T(1,128)} %broadcast_in_dim.89), calls=%async_computation.3 | async-start | bytes 32768 | tf_op jit(solution)/shard_map/all_to_all | solution.py:193
  16.6 145.0 %reduce-scatter.2.cloned.1.call-start = ((), (), s32[]{:S(2)}) async-start(), calls=%async_computation.5 | async-start | bytes 5242880 | tf_op jit(solution)/shard_map/reduce_scatter | solution.py:153
  28.6 25.0 %collective-permute-start.5 = (bf16[128,4096]{1,0:T(8,128)(2,1)S(1)}, bf16[128,4096]{1,0:T(8,128)(2,1)S(1)}, u32[]{:S(2)}, u32[]{:S(2)}) collective-permute-start(bf16[128,4096]{1,0:T(8,128)(2,1)S(1)} %convolution_convert_fusion.7), channel_id=1, source_target_pairs={{0,16},{4,20},{8,24},{12,28},{16,0},{20,4},{24,8},{28,12},{1,17},{... | collective-permute-start | bytes 3145736 | tf_op jit(solution)/shard_map/ppermute | solution.py:41
  29.2 25.0 %collective-permute-start.4 = (bf16[128,4096]{1,0:T(8,128)(2,1)S(1)}, bf16[128,4096]{1,0:T(8,128)(2,1)S(1)}, u32[]{:S(2)}, u32[]{:S(2)}) collective-permute-start(bf16[128,4096]{1,0:T(8,128)(2,1)S(1)} %convolution_convert_fusion.7), channel_id=1, source_target_pairs={{0,8},{4,12},{8,0},{12,4},{16,24},{20,28},{24,16},{28,20},{1,9},{5... | collective-permute-start | bytes 3145736 | tf_op jit(solution)/shard_map/ppermute | solution.py:41
  29.9 26.1 %collective-permute-start.3 = (bf16[128,4096]{1,0:T(8,128)(2,1)S(1)}, bf16[128,4096]{1,0:T(8,128)(2,1)}, u32[]{:S(2)}, u32[]{:S(2)}) collective-permute-start(bf16[128,4096]{1,0:T(8,128)(2,1)S(1)} %convolution_convert_fusion.7), channel_id=1, source_target_pairs={{0,4},{4,0},{8,12},{12,8},{16,20},{20,16},{24,28},{28,24},{1,5},{5... | collective-permute-start | bytes 3145736 | tf_op jit(solution)/shard_map/ppermute | solution.py:41
  53.7 12.9 %collective-permute-start.9 = (bf16[64,4096]{1,0:T(8,128)(2,1)S(1)}, bf16[64,4096]{1,0:T(8,128)(2,1)S(1)}, u32[]{:S(2)}, u32[]{:S(2)}) collective-permute-start(bf16[64,4096]{1,0:T(8,128)(2,1)S(1)} %slice.169), channel_id=1, source_target_pairs={{0,8},{4,12},{8,0},{12,4},{16,24},{20,28},{24,16},{28,20},{1,9},{5... | collective-permute-start | bytes 1572872 | tf_op jit(solution)/shard_map/ppermute | solution.py:41
  54.3 5.4 %copy-start.6 = (bf16[512,4096]{1,0:T(8,128)(2,1)S(1)}, bf16[512,4096]{1,0:T(8,128)(2,1)}, u32[]{:S(2)}) copy-start(bf16[512,4096]{1,0:T(8,128)(2,1)} %param.8) | copy-start | bytes 12582916
  54.3 12.6 %collective-permute-start.8 = (bf16[64,4096]{1,0:T(8,128)(2,1)S(1)}, bf16[64,4096]{1,0:T(8,128)(2,1)S(1)}, u32[]{:S(2)}, u32[]{:S(2)}) collective-permute-start(bf16[64,4096]{1,0:T(8,128)(2,1)S(1)} %slice.168), channel_id=1, source_target_pairs={{0,16},{4,20},{8,24},{12,28},{16,0},{20,4},{24,8},{28,12},{1,17},{... | collective-permute-start | bytes 1572872 | tf_op jit(solution)/shard_map/ppermute | solution.py:41
  55.5 4.2 %collective-permute-start.7 = (bf16[128,4096]{1,0:T(8,128)(2,1)S(1)}, bf16[128,4096]{1,0:T(8,128)(2,1)S(1)}, u32[]{:S(2)}, u32[]{:S(2)}) collective-permute-start(bf16[128,4096]{1,0:T(8,128)(2,1)S(1)} %collective-permute-done.5), channel_id=1, source_target_pairs={{0,4},{4,0},{8,12},{12,8},{16,20},{20,16},{24,28},{28,24},{1,5},{5... | collective-permute-start | bytes 3145736 | tf_op jit(solution)/shard_map/ppermute | solution.py:41
  55.5 4.2 %collective-permute-start.6 = (bf16[128,4096]{1,0:T(8,128)(2,1)S(1)}, bf16[128,4096]{1,0:T(8,128)(2,1)S(1)}, u32[]{:S(2)}, u32[]{:S(2)}) collective-permute-start(bf16[128,4096]{1,0:T(8,128)(2,1)S(1)} %collective-permute-done.4), channel_id=1, source_target_pairs={{0,4},{4,0},{8,12},{12,8},{16,20},{20,16},{24,28},{28,24},{1,5},{5... | collective-permute-start | bytes 3145736 | tf_op jit(solution)/shard_map/ppermute | solution.py:41
  67.1 4.0 %collective-permute-start.10 = (bf16[128,4096]{1,0:T(8,128)(2,1)S(1)}, bf16[128,4096]{1,0:T(8,128)(2,1)S(1)}, u32[]{:S(2)}, u32[]{:S(2)}) collective-permute-start(bf16[128,4096]{1,0:T(8,128)(2,1)S(1)} %get-tuple-element.65), channel_id=1, source_target_pairs={{0,4},{4,0},{8,12},{12,8},{16,20},{20,16},{24,28},{28,24},{1,5},{5... | collective-permute-start | bytes 3145736 | tf_op jit(solution)/shard_map/ppermute | solution.py:41
  67.2 13.1 %copy-start.4 = (s32[512]{0:T(512)}, s32[512]{0:T(512)S(1)}, u32[]{:S(2)}) copy-start(s32[512]{0:T(512)S(1)} %convert_add_fusion) | copy-start | bytes 6148
  72.5 7.9 %copy-start.2 = (f32[512]{0:T(512)S(1)}, f32[512]{0:T(512)}, u32[]{:S(2)}) copy-start(f32[512]{0:T(512)} %param.13) | copy-start | bytes 6148
  72.8 3.7 %collective-permute-start.13 = (f32[2,512]{1,0:T(2,128)S(1)}, f32[2,512]{1,0:T(2,128)S(1)}, u32[]{:S(2)}, u32[]{:S(2)}) collective-permute-start(f32[2,512]{1,0:T(2,128)S(1)} %pad_maximum_fusion.2), channel_id=1, source_target_pairs={{0,3},{1,0},{2,1},{3,2},{4,7},{5,4},{6,5},{7,6},{8,11},{9,8},{10,9... | collective-permute-start | bytes 12296 | tf_op jit(solution)/shard_map/ppermute | solution.py:32
  73.4 4.5 %collective-permute-start.12 = (f32[2,512]{1,0:T(2,128)S(1)}, f32[2,512]{1,0:T(2,128)S(1)}, u32[]{:S(2)}, u32[]{:S(2)}) collective-permute-start(f32[2,512]{1,0:T(2,128)S(1)} %pad_maximum_fusion.2), channel_id=1, source_target_pairs={{0,2},{1,3},{2,0},{3,1},{4,6},{5,7},{6,4},{7,5},{8,10},{9,11},{10,... | collective-permute-start | bytes 12296 | tf_op jit(solution)/shard_map/ppermute | solution.py:32
  74.9 5.4 %collective-permute-start.11 = (f32[2,512]{1,0:T(2,128)S(1)}, f32[2,512]{1,0:T(2,128)S(1)}, u32[]{:S(2)}, u32[]{:S(2)}) collective-permute-start(f32[2,512]{1,0:T(2,128)S(1)} %pad_maximum_fusion.2), channel_id=1, source_target_pairs={{0,1},{1,2},{2,3},{3,0},{4,5},{5,6},{6,7},{7,4},{8,9},{9,10},{10,1... | collective-permute-start | bytes 12296 | tf_op jit(solution)/shard_map/ppermute | solution.py:32
  87.4 11.9 %copy-start.7 = (bf16[512,4096]{1,0:T(8,128)(2,1)S(1)}, bf16[512,4096]{1,0:T(8,128)(2,1)}, u32[]{:S(2)}) copy-start(bf16[512,4096]{1,0:T(8,128)(2,1)} %param.8) | copy-start | bytes 12582916
  92.1 7.2 %collective-permute-start.14 = (bf16[512,4096]{1,0:T(8,128)(2,1)S(1)}, bf16[512,4096]{1,0:T(8,128)(2,1)S(1)}, u32[]{:S(2)}, u32[]{:S(2)}) collective-permute-start(bf16[512,4096]{1,0:T(8,128)(2,1)S(1)} %convolution_convert_fusion.5), channel_id=1, source_target_pairs={{0,4},{4,0},{8,12},{12,8},{16,20},{20,16},{24,28},{28,24},{1,5},{5... | collective-permute-start | bytes 12582920 | tf_op jit(solution)/shard_map/ppermute | solution.py:41
  101.7 17.4 %copy-start.1 = (bf16[512,4096]{1,0:T(8,128)(2,1)}, bf16[512,4096]{1,0:T(8,128)(2,1)S(1)}, u32[]{:S(2)}) copy-start(bf16[512,4096]{1,0:T(8,128)(2,1)S(1)} %add_convert_fusion) | copy-start | bytes 12582916
  103.0 14.8 %collective-permute-start.19 = (bf16[64,4096]{1,0:T(8,128)(2,1)S(1)}, bf16[64,4096]{1,0:T(8,128)(2,1)S(1)}, u32[]{:S(2)}, u32[]{:S(2)}) collective-permute-start(bf16[64,4096]{1,0:T(8,128)(2,1)S(1)} %get-tuple-element.69), channel_id=1, source_target_pairs={{0,8},{4,12},{8,0},{12,4},{16,24},{20,28},{24,16},{28,20},{1,9},{5... | collective-permute-start | bytes 1572872 | tf_op jit(solution)/shard_map/ppermute | solution.py:41
  104.2 14.8 %collective-permute-start.15 = (bf16[64,4096]{1,0:T(8,128)(2,1)S(1)}, bf16[64,4096]{1,0:T(8,128)(2,1)S(1)}, u32[]{:S(2)}, u32[]{:S(2)}) collective-permute-start(bf16[64,4096]{1,0:T(8,128)(2,1)S(1)} %get-tuple-element.71), channel_id=1, source_target_pairs={{0,16},{4,20},{8,24},{12,28},{16,0},{20,4},{24,8},{28,12},{1,17},{... | collective-permute-start | bytes 1572872 | tf_op jit(solution)/shard_map/ppermute | solution.py:41
  105.0 25.3 %collective-permute-start.18 = (bf16[64,4096]{1,0:T(8,128)(2,1)}, bf16[64,4096]{1,0:T(8,128)(2,1)S(1)}, u32[]{:S(2)}, u32[]{:S(2)}) collective-permute-start(bf16[64,4096]{1,0:T(8,128)(2,1)} %get-tuple-element.68), channel_id=1, source_target_pairs={{0,16},{4,20},{8,24},{12,28},{16,0},{20,4},{24,8},{28,12},{1,17},{... | collective-permute-start | bytes 1572872 | tf_op jit(solution)/shard_map/ppermute | solution.py:41
  106.3 24.0 %collective-permute-start.17 = (bf16[64,4096]{1,0:T(8,128)(2,1)}, bf16[64,4096]{1,0:T(8,128)(2,1)S(1)}, u32[]{:S(2)}, u32[]{:S(2)}) collective-permute-start(bf16[64,4096]{1,0:T(8,128)(2,1)} %get-tuple-element.70), channel_id=1, source_target_pairs={{0,8},{4,12},{8,0},{12,4},{16,24},{20,28},{24,16},{28,20},{1,9},{5... | collective-permute-start | bytes 1572872 | tf_op jit(solution)/shard_map/ppermute | solution.py:41
  119.3 42.2 %copy-start.3 = (f32[512]{0:T(512)S(1)}, f32[512]{0:T(512)}, u32[]{:S(2)}) copy-start(f32[512]{0:T(512)} %param.13) | copy-start | bytes 6148
  119.3 42.2 %copy-start.5 = (s32[512]{0:T(512)S(1)}, s32[512]{0:T(512)}, u32[]{:S(2)}) copy-start(s32[512]{0:T(512)} %copy-done.4) | copy-start | bytes 6148
  119.3 21.1 %collective-permute-start.20 = (bf16[64,4096]{1,0:T(8,128)(2,1)S(1)}, bf16[64,4096]{1,0:T(8,128)(2,1)S(1)}, u32[]{:S(2)}, u32[]{:S(2)}) collective-permute-start(bf16[64,4096]{1,0:T(8,128)(2,1)S(1)} %get-tuple-element.72), channel_id=1, source_target_pairs={{0,16},{4,20},{8,24},{12,28},{16,0},{20,4},{24,8},{28,12},{1,17},{... | collective-permute-start | bytes 1572872 | tf_op jit(solution)/shard_map/ppermute | solution.py:41
  120.1 20.3 %collective-permute-start.16 = (bf16[64,4096]{1,0:T(8,128)(2,1)S(1)}, bf16[64,4096]{1,0:T(8,128)(2,1)S(1)}, u32[]{:S(2)}, u32[]{:S(2)}) collective-permute-start(bf16[64,4096]{1,0:T(8,128)(2,1)S(1)} %get-tuple-element.73), channel_id=1, source_target_pairs={{0,8},{4,12},{8,0},{12,4},{16,24},{20,28},{24,16},{28,20},{1,9},{5... | collective-permute-start | bytes 1572872 | tf_op jit(solution)/shard_map/ppermute | solution.py:41
Sparse Core Ops, SparseCore 0:
  87.5 73.9 reduce-scatter.1

commit v2 on v1

--- a/solution.py
+++ b/solution.py
@@ -24,6 +24,10 @@
 
 def add_bf16(a, b):
     return (a.astype(F32) + b.astype(F32)).astype(BF16)
+
+
+def half_of(room):
+    return (room // 2 + 15) // 16 * 16
 
 
 def shift_gather(value, axis, size):
@@ -96,17 +100,9 @@
     ]
 
 
-def gather_cube(rows):
-    half = rows.shape[0] // 2
-    over_x = swap(rows, 2)
-    over_y = swap(rows, 4)
-    far = [swap(over_x[:half], 4), swap(over_y[half:], 2)]
-    return rows, over_x, over_y, far
-
-
 def scatter_cube(total):
     room = total.shape[0] // 4
-    half = room // 2
+    half = half_of(room)
     mine, to_x, to_y, far = [total[t * room:(t + 1) * room] for t in range(4)]
     far_first = swap(far[:half], 4)
     far_last = swap(far[half:], 2)
@@ -127,7 +123,8 @@
     pick = pick_rows(room, counts, rank, i_dp * n_neg + i_neg)
     rows = dot_f32(pick, passages, ((1,), (0,))).astype(BF16)
     rows = lax.optimization_barrier(rows)
-    rows, over_x, over_y, far = gather_cube(rows)
+    over_x = swap(rows, 2)
+    over_y = swap(rows, 4)
     over_core = swap(rows, 1)
 
     turn = jnp.arange(8, dtype=jnp.int32)
@@ -137,11 +134,16 @@
     groups, logits, column_ids = [], [], []
 
     def take(blocks, first, stop, step):
+        group_lift = lift[first:stop:step].reshape(-1)
+        if len(logits) == 2:
+            group_lift = once(logits[0], group_lift)
         groups.append(jnp.concatenate(blocks))
-        logits.append(logits_of(queries, groups[-1], lift[first:stop:step].reshape(-1)))
+        logits.append(logits_of(queries, groups[-1], group_lift))
         column_ids.append(slot_id[first:stop:step].reshape(-1))
 
     take([rows, over_core], 0, 5, 4)
+    half = half_of(room)
+    far = [swap(over_x[:half], 4), swap(over_y[half:], 2)]
     take([over_x, over_y], 1, 3, 1)
     take([swap(over_x, 1), swap(over_y, 1)], 5, 7, 1)
     far = once(logits[-1], jnp.concatenate(far))
@@ -214,14 +216,16 @@
         )
 
     _, longest = rank_rows(counts)
+    room = list_len
     if n_dp == 8:
-        grads = gradients_cube(list_len, queries, passages, counts, pos_id, row_weight, n_neg)
+        room = list_len - list_len // 8
+        grads = gradients_cube(room, queries, passages, counts, pos_id, row_weight, n_neg)
     else:
-        grads = plain(list_len)
+        grads = plain(room)
     _, query_grad, passage_grad = lax.while_loop(
         lambda state: state[0],
         lambda state: (jnp.zeros((), jnp.bool_), *plain(pass_rows)),
-        (longest > list_len, *grads),
+        (longest > room, *grads),
     )
     return query_grad, passage_grad
 

time: 169 us -> 184 us (1.089)
  matrix products: 28.3 us -> 39.1 us
  local copies, waits for them, and re-layouts: 5.59 us -> 15 us
  waiting for transfers between devices: 95.3 us -> 86.5 us
  other arithmetic: 3.47 us -> 5.8 us
    ppermute x15, waiting for transfers between devices: 66.4 us -> 45.3 us  [swap(): return lax.ppermute(value, 'dp', [(d, d ^ bit) for d in range(8)])]
    reduce_scatter x1, waiting for transfers between devices: 17.1 us -> 31.5 us  [gradients_cube(): lax.psum_scatter(query_part, 'neg', scatter_dimension=1, tiled=True)]
    dot_general x13, matrix products: 28.3 us -> 39.1 us  [dot_f32(): return lax.dot_general(a, b, (dims, ((), ())), preferred_element_type=F32)]
    unnamed x20, local copies, waits for them, and re-layouts: 1.68 us -> 7.5 us
    unnamed x1, other arithmetic: 0.17 us -> 2.66 us
    concatenate x1, local copies, waits for them, and re-layouts: 0.07 us -> 2.2 us  [gradients_cube(): columns = jnp.concatenate(groups)]
    ppermute x3, waiting for transfers between devices: 4.74 us -> 2.65 us  [shift_gather(): lax.ppermute(value, axis, [(j, (j + hop) % size) for j in range(size)])]
  transfers between devices with their start and end apart: 20 -> 20, of which waited for: 14 -> 9; matrix products, arithmetic and copies ran while one was open for 13% -> 23% of each run, Pallas kernels for 0% -> 0%
where the time goes in v2:
time: 184 us
  waiting for transfers between devices  86.5 us (47%)
  matrix products  39.1 us (21%)
  starting transfers between devices  19.9 us (11%)
  between operations  17.4 us (9%)
  local copies, waits for them, and re-layouts  15 us (8%)
  other arithmetic  5.8 us (3%)
    ppermute x15, waiting for transfers between devices, swap(): return lax.ppermute(value, 'dp', [(d, d ^ bit) for d in range(8)])  45.3 us
    dot_general x13, matrix products, dot_f32(): return lax.dot_general(a, b, (dims, ((), ())), preferred_element_type=F32)  39.1 us
    reduce_scatter x1, waiting for transfers between devices, gradients_cube(): lax.psum_scatter(query_part, 'neg', scatter_dimension=1, tiled=True)  31.5 us
    ppermute x15, starting transfers between devices, swap(): return lax.ppermute(value, 'dp', [(d, d ^ bit) for d in range(8)])  9.97 us
    unnamed x20, local copies, waits for them, and re-layouts  7.5 us
    all_to_all x1, starting transfers between devices, body(): lax.all_to_all(jnp.broadcast_to(packed, (devices, list_len)), ('neg', 'dp...  7.3 us
    all_to_all x1, waiting for transfers between devices, body(): lax.all_to_all(jnp.broadcast_to(packed, (devices, list_len)), ('neg', 'dp...  7 us
  transfers between devices with their start and end apart: 20, of which 9 were waited for; matrix products, arithmetic and copies ran while one was open for 23% of the time, Pallas kernels for 0%

profile of v2, /device:TPU:0, one launch (start us, length us, event | category | flops | bytes accessed | tf_op | source)
XLA Modules:
  0.0 183.7 jit_solution(548978187447001387)
XLA Ops:
  9.3 7.3 %all-to-all-start.3 = ((s32[32,1,128]{2,1,0:T(1,128)}), s32[32,1,128]{2,1,0:T(1,128)S(1)}, u32[]{:S(2)}, u32[]{:S(2)}) async-start(s32[32,1,128]{2,1,0:T(1,128)} %broadcast_in_dim.91), calls=%async_computation.3 | async-start | bytes 32768 | tf_op jit(solution)/shard_map/all_to_all | solution.py:195
  16.6 7.0 %all-to-all-done.3 = s32[32,1,128]{2,1,0:T(1,128)S(1)} async-done(((s32[32,1,128]{2,1,0:T(1,128)}), s32[32,1,128]{2,1,0:T(1,128)S(1)}, u32[]{:S(2)}, u32[]{:S(2)}) %all-to-all-start.3) | async-done | bytes 16416 | tf_op jit(solution)/shard_map/all_to_all | solution.py:195
  23.7 0.9 fusion.20
  26.6 2.0 %convolution_convert_fusion.7 = bf16[112,4096]{1,0:T(8,128)(2,1)S(1)} fusion(bf16[256,4096]{1,0:T(8,128)(2,1)} %param.9, s32[256]{0:T(256)S(1)} %bitcast.79, pred[256]{0:T(512)(128)(4,1)S(1)} %compare_reduce_fusion.1), kind=kOutput, calls=%fused_computation.53 | convolution fusion | flops 235397120 | bytes 3015936 | tf_op jit(solution)/shard_map/dot_general | solution.py:17
  30.5 1.0 constant_dynamic-update-slice_fusion.7
  31.5 19.3 %collective-permute-done.5 = bf16[112,4096]{1,0:T(8,128)(2,1)S(1)} collective-permute-done((bf16[112,4096]{1,0:T(8,128)(2,1)S(1)}, bf16[112,4096]{1,0:T(8,128)(2,1)S(1)}, u32[]{:S(2)}, u32[]{:S(2)}) %collective-permute-start.5) | collective-permute-done | bytes 917536 | tf_op jit(solution)/shard_map/ppermute | solution.py:45
  53.5 3.9 %fusion.148 = (f32[512]{0:T(512)S(1)}, f32[224,512]{1,0:T(8,128)S(1)}) fusion(f32[224]{0:T(256)S(1)} %add.345, bf16[512,4096]{1,0:T(8,128)(2,1)} %param.8, bf16[112,4096]{1,0:T(8,128)(2,1)} %collective-permute-done.3, bf16[112,4096]{1,0:T(8,128)(2,1)S(1)} %convolution_convert_fusion.7), kind=kOutput, calls=%fused_computation.241 | convolution fusion | flops 943537664 | bytes 6491008 | tf_op jit(solution)/shard_map/dot_general | solution.py:17
  59.7 2.5 %constant_dynamic-update-slice_fusion.6 = bf16[896,4096]{1,0:T(8,128)(2,1)} fusion(bf16[896,4096]{1,0:T(8,128)(2,1)} %constant_dynamic-update-slice_fusion.7, bf16[112,4096]{1,0:T(8,128)(2,1)} %collective-permute-done.3), kind=kLoop, calls=%fused_computation.158 | loop fusion | bytes 1835008
  62.2 1.0 constant_dynamic-update-slice_fusion.5
  63.2 1.0 constant_dynamic-update-slice_fusion.4
  64.2 1.0 constant_dynamic-update-slice_fusion.3
  65.2 1.5 fusion.147
  68.4 1.0 constant_dynamic-update-slice_fusion.2
  69.4 2.7 %constant_dynamic-update-slice_fusion.1 = (bf16[896,4096]{1,0:T(8,128)(2,1)}, bf16[112,4096]{1,0:T(8,128)(2,1)}) fusion(bf16[896,4096]{1,0:T(8,128)(2,1)} %constant_dynamic-update-slice_fusion.2, bf16[48,4096]{1,0:T(8,128)(2,1)} %collective-permute-done.9, bf16[64,4096]{1,0:T(8,128)(2,1)} %collective-permute-done.8, pred[]{:T(512)} %bitcast.15), kind=kLoop, calls=%fused_computation.153 | loop fusion | flops 2293760 | bytes 2753024
  73.3 3.8 %fusion.149 = (f32[512]{0:T(512)S(1)}, f32[224,512]{1,0:T(8,128)S(1)}) fusion(f32[224]{0:T(256)S(1)} %add.348, bf16[512,4096]{1,0:T(8,128)(2,1)} %param.8, bf16[112,4096]{1,0:T(8,128)(2,1)S(1)} %collective-permute-done.5, bf16[112,4096]{1,0:T(8,128)(2,1)S(1)} %collective-permute-done.4), kind=kOutput, calls=%fused_computation.242 | convolution fusion | flops 943537664 | bytes 6491008 | tf_op jit(solution)/shard_map/dot_general | solution.py:17
  77.1 2.9 %fusion.146 = (f32[512]{0:T(512)S(1)}, f32[224,512]{1,0:T(8,128)S(1)}) fusion(f32[224]{0:T(256)S(1)} %add.353, bf16[512,4096]{1,0:T(8,128)(2,1)S(1)} %copy-done.7, bf16[112,4096]{1,0:T(8,128)(2,1)} %collective-permute-done.10, bf16[112,4096]{1,0:T(8,128)(2,1)} %get-tuple-element.65), kind=kOutput, calls=%fused_computation.239 | convolution fusion | flops 943537664 | bytes 6491008 | tf_op jit(solution)/shard_map/dot_general | solution.py:17
  80.9 1.4 collective-permute-start.12
  82.9 2.2 %constant_dynamic-update-slice_fusion = bf16[896,4096]{1,0:T(8,128)(2,1)} fusion(bf16[896,4096]{1,0:T(8,128)(2,1)} %get-tuple-element.64, bf16[112,4096]{1,0:T(8,128)(2,1)} %collective-permute-done.10), kind=kLoop, calls=%fused_computation.152 | loop fusion | bytes 1835008 | tf_op jit(solution)/shard_map/concatenate | solution.py:151
  85.5 2.3 %collective-permute-done.11 = f32[2,512]{1,0:T(2,128)S(1)} collective-permute-done((f32[2,512]{1,0:T(2,128)S(1)}, f32[2,512]{1,0:T(2,128)S(1)}, u32[]{:S(2)}, u32[]{:S(2)}) %collective-permute-start.11) | collective-permute-done | bytes 4128 | tf_op jit(solution)/shard_map/ppermute | solution.py:36
  88.5 3.9 %convolution_convert_fusion.5 = bf16[448,4096]{1,0:T(8,128)(2,1)} fusion(bf16[512,4096]{1,0:T(8,128)(2,1)S(1)} %copy-done.7, bf16[112,512]{1,0:T(8,128)(2,1)S(1)} %get-tuple-element.73, bf16[224,512]{1,0:T(8,128)(2,1)S(1)} %get-tuple-element.77, bf16[112,512]{1,0:T(8,128)(2,1)S(1)} %get-tuple-element.74), kind=kOutput, calls=%fused_computation.51 | convolution fusion | flops 1882259456 | bytes 8323072 | tf_op jit(solution)/shard_map/dot_general | solution.py:17
  92.4 9.2 %convolution_convert_fusion.4 = bf16[512,4096]{1,0:T(8,128)(2,1)} fusion(bf16[896,512]{1,0:T(8,128)(2,1)S(1)} %pad_maximum_fusion.1, bf16[896,4096]{1,0:T(8,128)(2,1)} %constant_dynamic-update-slice_fusion), kind=kOutput, calls=%fused_computation.50 | convolution fusion | flops 3760193536 | bytes 12451840 | tf_op jit(solution)/shard_map/dot_general | solution.py:17
  101.6 5.4 %add_convert_fusion = bf16[448,4096]{1,0:T(8,128)(2,1)S(1)} fusion(bf16[448,4096]{1,0:T(8,128)(2,1)} %collective-permute-done.14, bf16[512,4096]{1,0:T(8,128)(2,1)} %param.8, bf16[112,512]{1,0:T(8,128)(2,1)S(1)} %get-tuple-element.75, bf16[224,512]{1,0:T(8,128)(2,1)S(1)} %get-tuple-element.76, bf16[112,512]{1,0:T(8,128)(2,1)S(1)} %get-tuple-element.72), kind=kOutput, calls=%fused_computation.49 | convolution fusion | flops 1889599488 | bytes 11993088 | tf_op jit(solution)/shard_map/dot_general | solution.py:17
  107.1 1.6 collective-permute-start.15
  108.7 1.4 collective-permute-start.19
  111.3 10.5 %collective-permute-done.15 = bf16[64,4096]{1,0:T(8,128)(2,1)S(1)} collective-permute-done((bf16[64,4096]{1,0:T(8,128)(2,1)S(1)}, bf16[64,4096]{1,0:T(8,128)(2,1)S(1)}, u32[]{:S(2)}, u32[]{:S(2)}) %collective-permute-start.15) | collective-permute-done | bytes 524320 | tf_op jit(solution)/shard_map/ppermute | solution.py:45
  122.0 1.5 collective-permute-start.16
  123.7 1.4 collective-permute-start.20
  125.8 3.4 %collective-permute-done.17 = bf16[48,4096]{1,0:T(8,128)(2,1)S(1)} collective-permute-done((bf16[48,4096]{1,0:T(8,128)(2,1)S(1)}, bf16[48,4096]{1,0:T(8,128)(2,1)S(1)}, u32[]{:S(2)}, u32[]{:S(2)}) %collective-permute-start.17) | collective-permute-done | bytes 393248 | tf_op jit(solution)/shard_map/ppermute | solution.py:45
  129.2 4.0 %collective-permute-done.18 = bf16[64,4096]{1,0:T(8,128)(2,1)S(1)} collective-permute-done((bf16[64,4096]{1,0:T(8,128)(2,1)S(1)}, bf16[64,4096]{1,0:T(8,128)(2,1)S(1)}, u32[]{:S(2)}, u32[]{:S(2)}) %collective-permute-start.18) | collective-permute-done | bytes 524320 | tf_op jit(solution)/shard_map/ppermute | solution.py:45
  133.1 8.1 %collective-permute-done.20 = bf16[48,4096]{1,0:T(8,128)(2,1)} collective-permute-done((bf16[48,4096]{1,0:T(8,128)(2,1)S(1)}, bf16[48,4096]{1,0:T(8,128)(2,1)}, u32[]{:S(2)}, u32[]{:S(2)}) %collective-permute-start.20) | collective-permute-done | bytes 393248 | tf_op jit(solution)/shard_map/ppermute | solution.py:45
  141.3 4.1 %fusion.64 = f32[256,4096]{1,0:T(8,128)} fusion(bf16[448,4096]{1,0:T(8,128)(2,1)} %copy-done.1, bf16[48,4096]{1,0:T(8,128)(2,1)S(1)} %collective-permute-done.17, bf16[64,4096]{1,0:T(8,128)(2,1)S(1)} %collective-permute-done.16, bf16[48,4096]{1,0:T(8,128)(2,1)} %collective-permute-done.20, bf16[64,4096]{1,0:T(8,128)(2,1)S(1)} %collective-permute-done.18, ...), kind=kOutput, calls=%fused_computation.88 | convolution fusion | flops 240443392 | bytes 6948096 | tf_op jit(solution)/shard_map/dot_general | solution.py:17
  145.3 31.5 %reduce-scatter.2.cloned.1.call-done = bf16[512,1024]{1,0:T(8,128)(2,1)} async-done(((bf16[512,4096]{1,0:T(8,128)(2,1)}), bf16[512,1024]{1,0:T(8,128)(2,1)}) %reduce-scatter.2.cloned.1.call-update) | async-done | bytes 1048592 | tf_op jit(solution)/shard_map/reduce_scatter | solution.py:155
  (97 shorter events, 15.6 us)
Async XLA Ops:
  9.3 14.4 %all-to-all-start.3 = ((s32[32,1,128]{2,1,0:T(1,128)}), s32[32,1,128]{2,1,0:T(1,128)S(1)}, u32[]{:S(2)}, u32[]{:S(2)}) async-start(s32[32,1,128]{2,1,0:T(1,128)} %broadcast_in_dim.91), calls=%async_computation.3 | async-start | bytes 32768 | tf_op jit(solution)/shard_map/all_to_all | solution.py:195
  16.6 160.3 %reduce-scatter.2.cloned.1.call-start = ((), (), s32[]{:S(2)}) async-start(), calls=%async_computation.5 | async-start | bytes 5242880 | tf_op jit(solution)/shard_map/reduce_scatter | solution.py:155
  28.7 22.2 %collective-permute-start.5 = (bf16[112,4096]{1,0:T(8,128)(2,1)S(1)}, bf16[112,4096]{1,0:T(8,128)(2,1)S(1)}, u32[]{:S(2)}, u32[]{:S(2)}) collective-permute-start(bf16[112,4096]{1,0:T(8,128)(2,1)S(1)} %convolution_convert_fusion.7), channel_id=1, source_target_pairs={{0,16},{4,20},{8,24},{12,28},{16,0},{20,4},{24,8},{28,12},{1,17},{... | collective-permute-start | bytes 2752520 | tf_op jit(solution)/shard_map/ppermute | solution.py:45
  29.3 22.9 %collective-permute-start.4 = (bf16[112,4096]{1,0:T(8,128)(2,1)S(1)}, bf16[112,4096]{1,0:T(8,128)(2,1)S(1)}, u32[]{:S(2)}, u32[]{:S(2)}) collective-permute-start(bf16[112,4096]{1,0:T(8,128)(2,1)S(1)} %convolution_convert_fusion.7), channel_id=1, source_target_pairs={{0,8},{4,12},{8,0},{12,4},{16,24},{20,28},{24,16},{28,20},{1,9},{5... | collective-permute-start | bytes 2752520 | tf_op jit(solution)/shard_map/ppermute | solution.py:45
  29.9 23.7 %collective-permute-start.3 = (bf16[112,4096]{1,0:T(8,128)(2,1)S(1)}, bf16[112,4096]{1,0:T(8,128)(2,1)}, u32[]{:S(2)}, u32[]{:S(2)}) collective-permute-start(bf16[112,4096]{1,0:T(8,128)(2,1)S(1)} %convolution_convert_fusion.7), channel_id=1, source_target_pairs={{0,4},{4,0},{8,12},{12,8},{16,20},{20,16},{24,28},{28,24},{1,5},{5... | collective-permute-start | bytes 2752520 | tf_op jit(solution)/shard_map/ppermute | solution.py:45
  51.6 17.7 %collective-permute-start.9 = (bf16[48,4096]{1,0:T(8,128)(2,1)}, bf16[48,4096]{1,0:T(8,128)(2,1)}, u32[]{:S(2)}, u32[]{:S(2)}) collective-permute-start(bf16[48,4096]{1,0:T(8,128)(2,1)} %slice.174), channel_id=1, source_target_pairs={{0,8},{4,12},{8,0},{12,4},{16,24},{20,28},{24,16},{28,20},{1,9},{5... | collective-permute-start | bytes 1179656 | tf_op jit(solution)/shard_map/ppermute | solution.py:45
  53.0 16.4 %collective-permute-start.8 = (bf16[64,4096]{1,0:T(8,128)(2,1)}, bf16[64,4096]{1,0:T(8,128)(2,1)}, u32[]{:S(2)}, u32[]{:S(2)}) collective-permute-start(bf16[64,4096]{1,0:T(8,128)(2,1)} %slice.173), channel_id=1, source_target_pairs={{0,16},{4,20},{8,24},{12,28},{16,0},{20,4},{24,8},{28,12},{1,17},{... | collective-permute-start | bytes 1572872 | tf_op jit(solution)/shard_map/ppermute | solution.py:45
  59.2 6.0 %copy-start.6 = (bf16[512,4096]{1,0:T(8,128)(2,1)S(1)}, bf16[512,4096]{1,0:T(8,128)(2,1)}, u32[]{:S(2)}) copy-start(bf16[512,4096]{1,0:T(8,128)(2,1)} %param.8) | copy-start | bytes 12582916
  59.2 6.0 %collective-permute-start.7 = (bf16[112,4096]{1,0:T(8,128)(2,1)S(1)}, bf16[112,4096]{1,0:T(8,128)(2,1)S(1)}, u32[]{:S(2)}, u32[]{:S(2)}) collective-permute-start(bf16[112,4096]{1,0:T(8,128)(2,1)S(1)} %collective-permute-done.5), channel_id=1, source_target_pairs={{0,4},{4,0},{8,12},{12,8},{16,20},{20,16},{24,28},{28,24},{1,5},{5... | collective-permute-start | bytes 2752520 | tf_op jit(solution)/shard_map/ppermute | solution.py:45
  59.2 5.0 %collective-permute-start.6 = (bf16[112,4096]{1,0:T(8,128)(2,1)S(1)}, bf16[112,4096]{1,0:T(8,128)(2,1)S(1)}, u32[]{:S(2)}, u32[]{:S(2)}) collective-permute-start(bf16[112,4096]{1,0:T(8,128)(2,1)S(1)} %collective-permute-done.4), channel_id=1, source_target_pairs={{0,4},{4,0},{8,12},{12,8},{16,20},{20,16},{24,28},{28,24},{1,5},{5... | collective-permute-start | bytes 2752520 | tf_op jit(solution)/shard_map/ppermute | solution.py:45
  72.0 5.0 %collective-permute-start.10 = (bf16[112,4096]{1,0:T(8,128)(2,1)}, bf16[112,4096]{1,0:T(8,128)(2,1)}, u32[]{:S(2)}, u32[]{:S(2)}) collective-permute-start(bf16[112,4096]{1,0:T(8,128)(2,1)} %get-tuple-element.65), channel_id=1, source_target_pairs={{0,4},{4,0},{8,12},{12,8},{16,20},{20,16},{24,28},{28,24},{1,5},{5... | collective-permute-start | bytes 2752520 | tf_op jit(solution)/shard_map/ppermute | solution.py:45
  73.2 14.7 %copy-start.4 = (s32[512]{0:T(512)}, s32[512]{0:T(512)S(1)}, u32[]{:S(2)}) copy-start(s32[512]{0:T(512)S(1)} %convert_add_fusion) | copy-start | bytes 6148
  73.3 3.8 %copy-start.7 = (bf16[512,4096]{1,0:T(8,128)(2,1)S(1)}, bf16[512,4096]{1,0:T(8,128)(2,1)}, u32[]{:S(2)}) copy-start(bf16[512,4096]{1,0:T(8,128)(2,1)} %param.8) | copy-start | bytes 12582916
  77.1 10.7 %copy-start.2 = (f32[512]{0:T(512)S(1)}, f32[512]{0:T(512)}, u32[]{:S(2)}) copy-start(f32[512]{0:T(512)} %param.13) | copy-start | bytes 6148
  80.3 4.8 %collective-permute-start.13 = (f32[2,512]{1,0:T(2,128)S(1)}, f32[2,512]{1,0:T(2,128)S(1)}, u32[]{:S(2)}, u32[]{:S(2)}) collective-permute-start(f32[2,512]{1,0:T(2,128)S(1)} %pad_maximum_fusion.2), channel_id=1, source_target_pairs={{0,3},{1,0},{2,1},{3,2},{4,7},{5,4},{6,5},{7,6},{8,11},{9,8},{10,9... | collective-permute-start | bytes 12296 | tf_op jit(solution)/shard_map/ppermute | solution.py:36
  80.9 4.5 %collective-permute-start.12 = (f32[2,512]{1,0:T(2,128)S(1)}, f32[2,512]{1,0:T(2,128)S(1)}, u32[]{:S(2)}, u32[]{:S(2)}) collective-permute-start(f32[2,512]{1,0:T(2,128)S(1)} %pad_maximum_fusion.2), channel_id=1, source_target_pairs={{0,2},{1,3},{2,0},{3,1},{4,6},{5,7},{6,4},{7,5},{8,10},{9,11},{10,... | collective-permute-start | bytes 12296 | tf_op jit(solution)/shard_map/ppermute | solution.py:36
  82.4 5.4 %collective-permute-start.11 = (f32[2,512]{1,0:T(2,128)S(1)}, f32[2,512]{1,0:T(2,128)S(1)}, u32[]{:S(2)}, u32[]{:S(2)}) collective-permute-start(f32[2,512]{1,0:T(2,128)S(1)} %pad_maximum_fusion.2), channel_id=1, source_target_pairs={{0,1},{1,2},{2,3},{3,0},{4,5},{5,6},{6,7},{7,4},{8,9},{9,10},{10,1... | collective-permute-start | bytes 12296 | tf_op jit(solution)/shard_map/ppermute | solution.py:36
  92.4 9.2 %collective-permute-start.14 = (bf16[448,4096]{1,0:T(8,128)(2,1)}, bf16[448,4096]{1,0:T(8,128)(2,1)}, u32[]{:S(2)}, u32[]{:S(2)}) collective-permute-start(bf16[448,4096]{1,0:T(8,128)(2,1)} %convolution_convert_fusion.5), channel_id=1, source_target_pairs={{0,4},{4,0},{8,12},{12,8},{16,20},{20,16},{24,28},{28,24},{1,5},{5... | collective-permute-start | bytes 11010056 | tf_op jit(solution)/shard_map/ppermute | solution.py:45
  107.0 16.6 %copy-start.1 = (bf16[448,4096]{1,0:T(8,128)(2,1)}, bf16[448,4096]{1,0:T(8,128)(2,1)S(1)}, u32[]{:S(2)}) copy-start(bf16[448,4096]{1,0:T(8,128)(2,1)S(1)} %add_convert_fusion) | copy-start | bytes 11010052
  107.1 14.8 %collective-permute-start.15 = (bf16[64,4096]{1,0:T(8,128)(2,1)S(1)}, bf16[64,4096]{1,0:T(8,128)(2,1)S(1)}, u32[]{:S(2)}, u32[]{:S(2)}) collective-permute-start(bf16[64,4096]{1,0:T(8,128)(2,1)S(1)} %get-tuple-element.69), channel_id=1, source_target_pairs={{0,16},{4,20},{8,24},{12,28},{16,0},{20,4},{24,8},{28,12},{1,17},{... | collective-permute-start | bytes 1572872 | tf_op jit(solution)/shard_map/ppermute | solution.py:45
  108.7 14.9 %collective-permute-start.19 = (bf16[48,4096]{1,0:T(8,128)(2,1)S(1)}, bf16[48,4096]{1,0:T(8,128)(2,1)S(1)}, u32[]{:S(2)}, u32[]{:S(2)}) collective-permute-start(bf16[48,4096]{1,0:T(8,128)(2,1)S(1)} %get-tuple-element.70), channel_id=1, source_target_pairs={{0,8},{4,12},{8,0},{12,4},{16,24},{20,28},{24,16},{28,20},{1,9},{5... | collective-permute-start | bytes 1179656 | tf_op jit(solution)/shard_map/ppermute | solution.py:45
  110.1 19.0 %collective-permute-start.17 = (bf16[48,4096]{1,0:T(8,128)(2,1)S(1)}, bf16[48,4096]{1,0:T(8,128)(2,1)S(1)}, u32[]{:S(2)}, u32[]{:S(2)}) collective-permute-start(bf16[48,4096]{1,0:T(8,128)(2,1)S(1)} %get-tuple-element.71), channel_id=1, source_target_pairs={{0,8},{4,12},{8,0},{12,4},{16,24},{20,28},{24,16},{28,20},{1,9},{5... | collective-permute-start | bytes 1179656 | tf_op jit(solution)/shard_map/ppermute | solution.py:45
  110.8 22.3 %collective-permute-start.18 = (bf16[64,4096]{1,0:T(8,128)(2,1)S(1)}, bf16[64,4096]{1,0:T(8,128)(2,1)S(1)}, u32[]{:S(2)}, u32[]{:S(2)}) collective-permute-start(bf16[64,4096]{1,0:T(8,128)(2,1)S(1)} %get-tuple-element.68), channel_id=1, source_target_pairs={{0,16},{4,20},{8,24},{12,28},{16,0},{20,4},{24,8},{28,12},{1,17},{... | collective-permute-start | bytes 1572872 | tf_op jit(solution)/shard_map/ppermute | solution.py:45
  122.0 54.8 %copy-start.3 = (f32[512]{0:T(512)S(1)}, f32[512]{0:T(512)}, u32[]{:S(2)}) copy-start(f32[512]{0:T(512)} %param.13) | copy-start | bytes 6148
  122.0 54.8 %copy-start.5 = (s32[512]{0:T(512)S(1)}, s32[512]{0:T(512)}, u32[]{:S(2)}) copy-start(s32[512]{0:T(512)} %copy-done.4) | copy-start | bytes 6148
  122.0 19.2 %collective-permute-start.16 = (bf16[64,4096]{1,0:T(8,128)(2,1)S(1)}, bf16[64,4096]{1,0:T(8,128)(2,1)S(1)}, u32[]{:S(2)}, u32[]{:S(2)}) collective-permute-start(bf16[64,4096]{1,0:T(8,128)(2,1)S(1)} %add_convert_fusion.2), channel_id=1, source_target_pairs={{0,8},{4,12},{8,0},{12,4},{16,24},{20,28},{24,16},{28,20},{1,9},{5... | collective-permute-start | bytes 1572872 | tf_op jit(solution)/shard_map/ppermute | solution.py:45
  123.7 17.6 %collective-permute-start.20 = (bf16[48,4096]{1,0:T(8,128)(2,1)S(1)}, bf16[48,4096]{1,0:T(8,128)(2,1)}, u32[]{:S(2)}, u32[]{:S(2)}) collective-permute-start(bf16[48,4096]{1,0:T(8,128)(2,1)S(1)} %add_convert_fusion.4), channel_id=1, source_target_pairs={{0,16},{4,20},{8,24},{12,28},{16,0},{20,4},{24,8},{28,12},{1,17},{... | collective-permute-start | bytes 1179656 | tf_op jit(solution)/shard_map/ppermute | solution.py:45
Sparse Core Ops, SparseCore 0:
  101.7 75.0 reduce-scatter.1

commit v3 on v1

--- a/solution.py
+++ b/solution.py
@@ -137,8 +137,11 @@
     groups, logits, column_ids = [], [], []
 
     def take(blocks, first, stop, step):
+        group_lift = lift[first:stop:step].reshape(-1)
+        if len(logits) == 2:
+            group_lift = once(logits[0], group_lift)
         groups.append(jnp.concatenate(blocks))
-        logits.append(logits_of(queries, groups[-1], lift[first:stop:step].reshape(-1)))
+        logits.append(logits_of(queries, groups[-1], group_lift))
         column_ids.append(slot_id[first:stop:step].reshape(-1))
 
     take([rows, over_core], 0, 5, 4)

time: 169 us -> 176 us (1.041)
  local copies, waits for them, and re-layouts: 5.59 us -> 10.7 us
  waiting for transfers between devices: 95.3 us -> 90.9 us
  matrix products: 28.3 us -> 32.3 us
    dot_general x13, matrix products: 28.3 us -> 32.3 us  [dot_f32(): return lax.dot_general(a, b, (dims, ((), ())), preferred_element_type=F32)]
    ppermute x15, waiting for transfers between devices: 66.4 us -> 62.6 us  [swap(): return lax.ppermute(value, 'dp', [(d, d ^ bit) for d in range(8)])]
    unnamed x20 -> x32, local copies, waits for them, and re-layouts: 1.68 us -> 4.98 us
  transfers between devices with their start and end apart: 20 -> 20, of which waited for: 14 -> 11; matrix products, arithmetic and copies ran while one was open for 13% -> 15% of each run, Pallas kernels for 0% -> 0%
where the time goes in v3:
time: 176 us
  waiting for transfers between devices  90.9 us (52%)
  matrix products  32.3 us (18%)
  starting transfers between devices  19.8 us (11%)
  between operations  17.7 us (10%)
  local copies, waits for them, and re-layouts  10.7 us (6%)
  other arithmetic  4.55 us (3%)
    ppermute x15, waiting for transfers between devices, swap(): return lax.ppermute(value, 'dp', [(d, d ^ bit) for d in range(8)])  62.6 us
    dot_general x13, matrix products, dot_f32(): return lax.dot_general(a, b, (dims, ((), ())), preferred_element_type=F32)  32.3 us
    reduce_scatter x1, waiting for transfers between devices, gradients_cube(): lax.psum_scatter(query_part, 'neg', scatter_dimension=1, tiled=True)  17.9 us
    ppermute x15, starting transfers between devices, swap(): return lax.ppermute(value, 'dp', [(d, d ^ bit) for d in range(8)])  9.94 us
    all_to_all x1, starting transfers between devices, body(): lax.all_to_all(jnp.broadcast_to(packed, (devices, list_len)), ('neg', 'dp...  7.3 us
    all_to_all x1, waiting for transfers between devices, body(): lax.all_to_all(jnp.broadcast_to(packed, (devices, list_len)), ('neg', 'dp...  7 us
    unnamed x32, local copies, waits for them, and re-layouts  4.98 us
  transfers between devices with their start and end apart: 20, of which 11 were waited for; matrix products, arithmetic and copies ran while one was open for 15% of the time, Pallas kernels for 0%

profile of v3, /device:TPU:0, one launch (start us, length us, event | category | flops | bytes accessed | tf_op | source)
XLA Modules:
  0.0 175.9 jit_solution(6293282055094423650)
XLA Ops:
  9.3 7.3 %all-to-all-start.3 = ((s32[32,1,128]{2,1,0:T(1,128)}), s32[32,1,128]{2,1,0:T(1,128)S(1)}, u32[]{:S(2)}, u32[]{:S(2)}) async-start(s32[32,1,128]{2,1,0:T(1,128)} %broadcast_in_dim.91), calls=%async_computation.3 | async-start | bytes 32768 | tf_op jit(solution)/shard_map/all_to_all | solution.py:196
  16.6 7.0 %all-to-all-done.3 = s32[32,1,128]{2,1,0:T(1,128)S(1)} async-done(((s32[32,1,128]{2,1,0:T(1,128)}), s32[32,1,128]{2,1,0:T(1,128)S(1)}, u32[]{:S(2)}, u32[]{:S(2)}) %all-to-all-start.3) | async-done | bytes 16416 | tf_op jit(solution)/shard_map/all_to_all | solution.py:196
  26.5 2.0 %convolution_convert_fusion.7 = bf16[128,4096]{1,0:T(8,128)(2,1)S(1)} fusion(bf16[256,4096]{1,0:T(8,128)(2,1)} %param.9, s32[256]{0:T(256)S(1)} %bitcast.93, pred[256]{0:T(512)(128)(4,1)S(1)} %compare_reduce_fusion.1), kind=kOutput, calls=%fused_computation.53 | convolution fusion | flops 269025280 | bytes 3147008 | tf_op jit(solution)/shard_map/dot_general | solution.py:17
  30.5 23.1 %collective-permute-done.5 = bf16[128,4096]{1,0:T(8,128)(2,1)S(1)} collective-permute-done((bf16[128,4096]{1,0:T(8,128)(2,1)S(1)}, bf16[128,4096]{1,0:T(8,128)(2,1)S(1)}, u32[]{:S(2)}, u32[]{:S(2)}) %collective-permute-start.5) | collective-permute-done | bytes 1048608 | tf_op jit(solution)/shard_map/ppermute | solution.py:41
  54.3 1.2 collective-permute-start.8
  55.5 2.5 %fusion.145 = (f32[512]{0:T(512)S(1)}, f32[256,512]{1,0:T(8,128)S(1)}) fusion(f32[256]{0:T(256)S(1)} %bitcast.103, bf16[512,4096]{1,0:T(8,128)(2,1)S(1)} %copy-done.9, bf16[128,4096]{1,0:T(8,128)(2,1)} %collective-permute-done.3, bf16[128,4096]{1,0:T(8,128)(2,1)S(1)} %convolution_convert_fusion.7), kind=kOutput, calls=%fused_computation.241 | convolution fusion | flops 1078328832 | bytes 6818816 | tf_op jit(solution)/shard_map/dot_general | solution.py:17
  60.4 1.3 constant_dynamic-update-slice_fusion.6
  61.9 2.2 %collective-permute-done.6 = bf16[128,4096]{1,0:T(8,128)(2,1)S(1)} collective-permute-done((bf16[128,4096]{1,0:T(8,128)(2,1)S(1)}, bf16[128,4096]{1,0:T(8,128)(2,1)S(1)}, u32[]{:S(2)}, u32[]{:S(2)}) %collective-permute-start.6) | collective-permute-done | bytes 1048608 | tf_op jit(solution)/shard_map/ppermute | solution.py:41
  64.2 1.3 fusion.144
  67.4 1.2 constant_dynamic-update-slice_fusion.1
  68.7 3.2 %copy-done.4 = bf16[1024,4096]{1,0:T(8,128)(2,1)} copy-done((bf16[1024,4096]{1,0:T(8,128)(2,1)}, bf16[1024,4096]{1,0:T(8,128)(2,1)S(1)}, u32[]{:S(2)}) %copy-start.4) | copy-done | bytes 8388632
  72.8 3.6 %fusion.146 = (f32[512]{0:T(512)S(1)}, f32[256,512]{1,0:T(8,128)S(1)}) fusion(f32[256]{0:T(256)S(1)} %get-tuple-element.96, bf16[512,4096]{1,0:T(8,128)(2,1)} %param.8, bf16[128,4096]{1,0:T(8,128)(2,1)S(1)} %collective-permute-done.5, bf16[128,4096]{1,0:T(8,128)(2,1)S(1)} %collective-permute-done.4), kind=kOutput, calls=%fused_computation.242 | convolution fusion | flops 1078328832 | bytes 6818816 | tf_op jit(solution)/shard_map/dot_general | solution.py:17
  76.5 3.0 %fusion.143 = (f32[512]{0:T(512)S(1)}, f32[256,512]{1,0:T(8,128)S(1)}) fusion(f32[256]{0:T(256)S(1)} %bitcast.104, bf16[512,4096]{1,0:T(8,128)(2,1)S(1)} %copy-done.10, bf16[128,4096]{1,0:T(8,128)(2,1)} %collective-permute-done.10, bf16[128,4096]{1,0:T(8,128)(2,1)} %get-tuple-element.65), kind=kOutput, calls=%fused_computation.239 | convolution fusion | flops 1078328832 | bytes 6818816 | tf_op jit(solution)/shard_map/dot_general | solution.py:17
  80.4 1.4 collective-permute-start.12
  82.4 1.3 constant_dynamic-update-slice_fusion
  83.8 1.2 collective-permute-done.12
  84.9 2.3 %collective-permute-done.11 = f32[2,512]{1,0:T(2,128)S(1)} collective-permute-done((f32[2,512]{1,0:T(2,128)S(1)}, f32[2,512]{1,0:T(2,128)S(1)}, u32[]{:S(2)}, u32[]{:S(2)}) %collective-permute-start.11) | collective-permute-done | bytes 4128 | tf_op jit(solution)/shard_map/ppermute | solution.py:32
  88.0 6.4 %convolution_convert_fusion.4 = bf16[512,4096]{1,0:T(8,128)(2,1)} fusion(bf16[1024,512]{1,0:T(8,128)(2,1)S(1)} %pad_maximum_fusion.1, bf16[1024,4096]{1,0:T(8,128)(2,1)S(1)} %constant_dynamic-update-slice_fusion), kind=kOutput, calls=%fused_computation.50 | convolution fusion | flops 4297064448 | bytes 13631488 | tf_op jit(solution)/shard_map/dot_general | solution.py:17
  94.4 4.7 %convolution_convert_fusion.5 = bf16[512,4096]{1,0:T(8,128)(2,1)S(1)} fusion(bf16[512,4096]{1,0:T(8,128)(2,1)} %param.8, bf16[128,512]{1,0:T(8,128)(2,1)S(1)} %get-tuple-element.75, bf16[256,512]{1,0:T(8,128)(2,1)S(1)} %get-tuple-element.79, bf16[128,512]{1,0:T(8,128)(2,1)S(1)} %get-tuple-element.76), kind=kOutput, calls=%fused_computation.51 | convolution fusion | flops 2151153664 | bytes 8912896 | tf_op jit(solution)/shard_map/dot_general | solution.py:17
  99.2 7.1 %collective-permute-done.14 = bf16[512,4096]{1,0:T(8,128)(2,1)S(1)} collective-permute-done((bf16[512,4096]{1,0:T(8,128)(2,1)S(1)}, bf16[512,4096]{1,0:T(8,128)(2,1)S(1)}, u32[]{:S(2)}, u32[]{:S(2)}) %collective-permute-start.14) | collective-permute-done | bytes 4194336 | tf_op jit(solution)/shard_map/ppermute | solution.py:41
  106.3 2.3 %add_convert_fusion = bf16[512,4096]{1,0:T(8,128)(2,1)S(1)} fusion(bf16[512,4096]{1,0:T(8,128)(2,1)S(1)} %collective-permute-done.14, bf16[512,4096]{1,0:T(8,128)(2,1)S(1)} %copy-done.11, bf16[128,512]{1,0:T(8,128)(2,1)S(1)} %get-tuple-element.77, bf16[256,512]{1,0:T(8,128)(2,1)S(1)} %get-tuple-element.78, bf16[128,512]{1,0:T(8,128)(2,1)S(1)} %get-tuple-element.74), kind=kOutput, calls=%fused_computation.49 | convolution fusion | flops 2159542272 | bytes 13107200 | tf_op jit(solution)/shard_map/dot_general | solution.py:17
  108.7 1.3 fusion.137
  110.0 1.0 collective-permute-start.19
  111.1 1.4 collective-permute-start.15
  113.1 1.0 collective-permute-start.17
  114.1 10.7 %collective-permute-done.19 = bf16[64,4096]{1,0:T(8,128)(2,1)S(1)} collective-permute-done((bf16[64,4096]{1,0:T(8,128)(2,1)S(1)}, bf16[64,4096]{1,0:T(8,128)(2,1)S(1)}, u32[]{:S(2)}, u32[]{:S(2)}) %collective-permute-start.19) | collective-permute-done | bytes 524320 | tf_op jit(solution)/shard_map/ppermute | solution.py:41
  124.8 1.1 collective-permute-done.15
  126.1 1.4 collective-permute-start.20
  128.8 8.3 %collective-permute-done.18 = bf16[64,4096]{1,0:T(8,128)(2,1)S(1)} collective-permute-done((bf16[64,4096]{1,0:T(8,128)(2,1)}, bf16[64,4096]{1,0:T(8,128)(2,1)S(1)}, u32[]{:S(2)}, u32[]{:S(2)}) %collective-permute-start.18) | collective-permute-done | bytes 524320 | tf_op jit(solution)/shard_map/ppermute | solution.py:41
  137.1 10.1 %collective-permute-done.20 = bf16[64,4096]{1,0:T(8,128)(2,1)S(1)} collective-permute-done((bf16[64,4096]{1,0:T(8,128)(2,1)S(1)}, bf16[64,4096]{1,0:T(8,128)(2,1)S(1)}, u32[]{:S(2)}, u32[]{:S(2)}) %collective-permute-start.20) | collective-permute-done | bytes 524320 | tf_op jit(solution)/shard_map/ppermute | solution.py:41
  147.2 4.0 %fusion.64 = f32[256,4096]{1,0:T(8,128)} fusion(bf16[512,4096]{1,0:T(8,128)(2,1)} %copy-done.1, bf16[64,4096]{1,0:T(8,128)(2,1)S(1)} %collective-permute-done.17, bf16[64,4096]{1,0:T(8,128)(2,1)S(1)} %collective-permute-done.16, bf16[64,4096]{1,0:T(8,128)(2,1)S(1)} %collective-permute-done.20, bf16[64,4096]{1,0:T(8,128)(2,1)S(1)} %collective-permute-done.18, ...), kind=kOutput, calls=%fused_computation.87 | convolution fusion | flops 274792448 | bytes 7341312 | tf_op jit(solution)/shard_map/dot_general | solution.py:17
  151.2 17.9 %reduce-scatter.2.cloned.1.call-done = bf16[512,1024]{1,0:T(8,128)(2,1)} async-done(((bf16[512,4096]{1,0:T(8,128)(2,1)}), bf16[512,1024]{1,0:T(8,128)(2,1)}) %reduce-scatter.2.cloned.1.call-update) | async-done | bytes 1048592 | tf_op jit(solution)/shard_map/reduce_scatter | solution.py:156
  (100 shorter events, 14.3 us)
Async XLA Ops:
  9.3 14.4 %all-to-all-start.3 = ((s32[32,1,128]{2,1,0:T(1,128)}), s32[32,1,128]{2,1,0:T(1,128)S(1)}, u32[]{:S(2)}, u32[]{:S(2)}) async-start(s32[32,1,128]{2,1,0:T(1,128)} %broadcast_in_dim.91), calls=%async_computation.3 | async-start | bytes 32768 | tf_op jit(solution)/shard_map/all_to_all | solution.py:196
  16.6 152.5 %reduce-scatter.2.cloned.1.call-start = ((), (), s32[]{:S(2)}) async-start(), calls=%async_computation.5 | async-start | bytes 5242880 | tf_op jit(solution)/shard_map/reduce_scatter | solution.py:156
  28.6 25.0 %collective-permute-start.5 = (bf16[128,4096]{1,0:T(8,128)(2,1)S(1)}, bf16[128,4096]{1,0:T(8,128)(2,1)S(1)}, u32[]{:S(2)}, u32[]{:S(2)}) collective-permute-start(bf16[128,4096]{1,0:T(8,128)(2,1)S(1)} %convolution_convert_fusion.7), channel_id=1, source_target_pairs={{0,16},{4,20},{8,24},{12,28},{16,0},{20,4},{24,8},{28,12},{1,17},{... | collective-permute-start | bytes 3145736 | tf_op jit(solution)/shard_map/ppermute | solution.py:41
  29.2 25.0 %collective-permute-start.4 = (bf16[128,4096]{1,0:T(8,128)(2,1)S(1)}, bf16[128,4096]{1,0:T(8,128)(2,1)S(1)}, u32[]{:S(2)}, u32[]{:S(2)}) collective-permute-start(bf16[128,4096]{1,0:T(8,128)(2,1)S(1)} %convolution_convert_fusion.7), channel_id=1, source_target_pairs={{0,8},{4,12},{8,0},{12,4},{16,24},{20,28},{24,16},{28,20},{1,9},{5... | collective-permute-start | bytes 3145736 | tf_op jit(solution)/shard_map/ppermute | solution.py:41
  29.8 25.6 %collective-permute-start.3 = (bf16[128,4096]{1,0:T(8,128)(2,1)S(1)}, bf16[128,4096]{1,0:T(8,128)(2,1)}, u32[]{:S(2)}, u32[]{:S(2)}) collective-permute-start(bf16[128,4096]{1,0:T(8,128)(2,1)S(1)} %convolution_convert_fusion.7), channel_id=1, source_target_pairs={{0,4},{4,0},{8,12},{12,8},{16,20},{20,16},{24,28},{28,24},{1,5},{5... | collective-permute-start | bytes 3145736 | tf_op jit(solution)/shard_map/ppermute | solution.py:41
  30.1 25.3 %copy-start.9 = (bf16[512,4096]{1,0:T(8,128)(2,1)S(1)}, bf16[512,4096]{1,0:T(8,128)(2,1)}, u32[]{:S(2)}) copy-start(bf16[512,4096]{1,0:T(8,128)(2,1)} %param.8) | copy-start | bytes 12582916
  53.6 13.8 %collective-permute-start.9 = (bf16[64,4096]{1,0:T(8,128)(2,1)S(1)}, bf16[64,4096]{1,0:T(8,128)(2,1)S(1)}, u32[]{:S(2)}, u32[]{:S(2)}) collective-permute-start(bf16[64,4096]{1,0:T(8,128)(2,1)S(1)} %slice.174), channel_id=1, source_target_pairs={{0,8},{4,12},{8,0},{12,4},{16,24},{20,28},{24,16},{28,20},{1,9},{5... | collective-permute-start | bytes 1572872 | tf_op jit(solution)/shard_map/ppermute | solution.py:41
  54.3 13.1 %collective-permute-start.8 = (bf16[64,4096]{1,0:T(8,128)(2,1)S(1)}, bf16[64,4096]{1,0:T(8,128)(2,1)S(1)}, u32[]{:S(2)}, u32[]{:S(2)}) collective-permute-start(bf16[64,4096]{1,0:T(8,128)(2,1)S(1)} %slice.173), channel_id=1, source_target_pairs={{0,16},{4,20},{8,24},{12,28},{16,0},{20,4},{24,8},{28,12},{1,17},{... | collective-permute-start | bytes 1572872 | tf_op jit(solution)/shard_map/ppermute | solution.py:41
  58.0 6.2 %copy-start.2 = (f32[256,512]{1,0:T(8,128)}, f32[256,512]{1,0:T(8,128)S(1)}, u32[]{:S(2)}) copy-start(f32[256,512]{1,0:T(8,128)S(1)} %get-tuple-element.108) | copy-start | bytes 1572868
  59.8 4.3 %collective-permute-start.7 = (bf16[128,4096]{1,0:T(8,128)(2,1)S(1)}, bf16[128,4096]{1,0:T(8,128)(2,1)S(1)}, u32[]{:S(2)}, u32[]{:S(2)}) collective-permute-start(bf16[128,4096]{1,0:T(8,128)(2,1)S(1)} %collective-permute-done.5), channel_id=1, source_target_pairs={{0,4},{4,0},{8,12},{12,8},{16,20},{20,16},{24,28},{28,24},{1,5},{5... | collective-permute-start | bytes 3145736 | tf_op jit(solution)/shard_map/ppermute | solution.py:41
  59.9 4.1 %collective-permute-start.6 = (bf16[128,4096]{1,0:T(8,128)(2,1)S(1)}, bf16[128,4096]{1,0:T(8,128)(2,1)S(1)}, u32[]{:S(2)}, u32[]{:S(2)}) collective-permute-start(bf16[128,4096]{1,0:T(8,128)(2,1)S(1)} %collective-permute-done.4), channel_id=1, source_target_pairs={{0,4},{4,0},{8,12},{12,8},{16,20},{20,16},{24,28},{28,24},{1,5},{5... | collective-permute-start | bytes 3145736 | tf_op jit(solution)/shard_map/ppermute | solution.py:41
  68.7 3.2 %copy-start.4 = (bf16[1024,4096]{1,0:T(8,128)(2,1)}, bf16[1024,4096]{1,0:T(8,128)(2,1)S(1)}, u32[]{:S(2)}) copy-start(bf16[1024,4096]{1,0:T(8,128)(2,1)S(1)} %get-tuple-element.64) | copy-start | bytes 25165828
  71.9 4.5 %collective-permute-start.10 = (bf16[128,4096]{1,0:T(8,128)(2,1)}, bf16[128,4096]{1,0:T(8,128)(2,1)}, u32[]{:S(2)}, u32[]{:S(2)}) collective-permute-start(bf16[128,4096]{1,0:T(8,128)(2,1)} %get-tuple-element.65), channel_id=1, source_target_pairs={{0,4},{4,0},{8,12},{12,8},{16,20},{20,16},{24,28},{28,24},{1,5},{5... | collective-permute-start | bytes 3145736 | tf_op jit(solution)/shard_map/ppermute | solution.py:41
  72.7 14.5 %copy-start.7 = (s32[512]{0:T(512)}, s32[512]{0:T(512)S(1)}, u32[]{:S(2)}) copy-start(s32[512]{0:T(512)S(1)} %convert_add_fusion) | copy-start | bytes 6148
  72.8 3.7 %copy-start.10 = (bf16[512,4096]{1,0:T(8,128)(2,1)S(1)}, bf16[512,4096]{1,0:T(8,128)(2,1)}, u32[]{:S(2)}) copy-start(bf16[512,4096]{1,0:T(8,128)(2,1)} %param.8) | copy-start | bytes 12582916
  72.8 9.7 %slice-start = ((s8[8388608]{0:T(1024)(128)(4,1)}), s8[4194304]{0:T(1024)(128)(4,1)S(1)}, s32[]{:S(2)}) async-start(s8[8388608]{0:T(1024)(128)(4,1)} %bitcast.84), calls=%async_computation.6 | async-start | bytes 8388608
  76.5 6.0 %slice-start.1 = ((s8[8388608]{0:T(1024)(128)(4,1)}), s8[4194304]{0:T(1024)(128)(4,1)S(1)}, s32[]{:S(2)}) async-start(s8[8388608]{0:T(1024)(128)(4,1)} %bitcast.84), calls=%async_computation.7 | async-start | bytes 8388608
  79.5 7.8 %copy-start.5 = (f32[512]{0:T(512)S(1)}, f32[512]{0:T(512)}, u32[]{:S(2)}) copy-start(f32[512]{0:T(512)} %param.13) | copy-start | bytes 6148
  79.9 3.9 %collective-permute-start.13 = (f32[2,512]{1,0:T(2,128)S(1)}, f32[2,512]{1,0:T(2,128)S(1)}, u32[]{:S(2)}, u32[]{:S(2)}) collective-permute-start(f32[2,512]{1,0:T(2,128)S(1)} %pad_maximum_fusion.2), channel_id=1, source_target_pairs={{0,3},{1,0},{2,1},{3,2},{4,7},{5,4},{6,5},{7,6},{8,11},{9,8},{10,9... | collective-permute-start | bytes 12296 | tf_op jit(solution)/shard_map/ppermute | solution.py:32
  80.4 4.5 %collective-permute-start.12 = (f32[2,512]{1,0:T(2,128)S(1)}, f32[2,512]{1,0:T(2,128)S(1)}, u32[]{:S(2)}, u32[]{:S(2)}) collective-permute-start(f32[2,512]{1,0:T(2,128)S(1)} %pad_maximum_fusion.2), channel_id=1, source_target_pairs={{0,2},{1,3},{2,0},{3,1},{4,6},{5,7},{6,4},{7,5},{8,10},{9,11},{10,... | collective-permute-start | bytes 12296 | tf_op jit(solution)/shard_map/ppermute | solution.py:32
  81.8 5.4 %collective-permute-start.11 = (f32[2,512]{1,0:T(2,128)S(1)}, f32[2,512]{1,0:T(2,128)S(1)}, u32[]{:S(2)}, u32[]{:S(2)}) collective-permute-start(f32[2,512]{1,0:T(2,128)S(1)} %pad_maximum_fusion.2), channel_id=1, source_target_pairs={{0,1},{1,2},{2,3},{3,0},{4,5},{5,6},{6,7},{7,4},{8,9},{9,10},{10,1... | collective-permute-start | bytes 12296 | tf_op jit(solution)/shard_map/ppermute | solution.py:32
  94.4 11.9 %copy-start.11 = (bf16[512,4096]{1,0:T(8,128)(2,1)S(1)}, bf16[512,4096]{1,0:T(8,128)(2,1)}, u32[]{:S(2)}) copy-start(bf16[512,4096]{1,0:T(8,128)(2,1)} %param.8) | copy-start | bytes 12582916
  99.1 7.2 %collective-permute-start.14 = (bf16[512,4096]{1,0:T(8,128)(2,1)S(1)}, bf16[512,4096]{1,0:T(8,128)(2,1)S(1)}, u32[]{:S(2)}, u32[]{:S(2)}) collective-permute-start(bf16[512,4096]{1,0:T(8,128)(2,1)S(1)} %convolution_convert_fusion.5), channel_id=1, source_target_pairs={{0,4},{4,0},{8,12},{12,8},{16,20},{20,16},{24,28},{28,24},{1,5},{5... | collective-permute-start | bytes 12582920 | tf_op jit(solution)/shard_map/ppermute | solution.py:41
  108.7 17.2 %copy-start.1 = (bf16[512,4096]{1,0:T(8,128)(2,1)}, bf16[512,4096]{1,0:T(8,128)(2,1)S(1)}, u32[]{:S(2)}) copy-start(bf16[512,4096]{1,0:T(8,128)(2,1)S(1)} %add_convert_fusion) | copy-start | bytes 12582916
  110.0 14.8 %collective-permute-start.19 = (bf16[64,4096]{1,0:T(8,128)(2,1)S(1)}, bf16[64,4096]{1,0:T(8,128)(2,1)S(1)}, u32[]{:S(2)}, u32[]{:S(2)}) collective-permute-start(bf16[64,4096]{1,0:T(8,128)(2,1)S(1)} %get-tuple-element.69), channel_id=1, source_target_pairs={{0,8},{4,12},{8,0},{12,4},{16,24},{20,28},{24,16},{28,20},{1,9},{5... | collective-permute-start | bytes 1572872 | tf_op jit(solution)/shard_map/ppermute | solution.py:41
  111.1 14.8 %collective-permute-start.15 = (bf16[64,4096]{1,0:T(8,128)(2,1)S(1)}, bf16[64,4096]{1,0:T(8,128)(2,1)S(1)}, u32[]{:S(2)}, u32[]{:S(2)}) collective-permute-start(bf16[64,4096]{1,0:T(8,128)(2,1)S(1)} %get-tuple-element.71), channel_id=1, source_target_pairs={{0,16},{4,20},{8,24},{12,28},{16,0},{20,4},{24,8},{28,12},{1,17},{... | collective-permute-start | bytes 1572872 | tf_op jit(solution)/shard_map/ppermute | solution.py:41
  112.4 24.7 %collective-permute-start.18 = (bf16[64,4096]{1,0:T(8,128)(2,1)}, bf16[64,4096]{1,0:T(8,128)(2,1)S(1)}, u32[]{:S(2)}, u32[]{:S(2)}) collective-permute-start(bf16[64,4096]{1,0:T(8,128)(2,1)} %get-tuple-element.68), channel_id=1, source_target_pairs={{0,16},{4,20},{8,24},{12,28},{16,0},{20,4},{24,8},{28,12},{1,17},{... | collective-permute-start | bytes 1572872 | tf_op jit(solution)/shard_map/ppermute | solution.py:41
  113.1 24.0 %collective-permute-start.17 = (bf16[64,4096]{1,0:T(8,128)(2,1)}, bf16[64,4096]{1,0:T(8,128)(2,1)S(1)}, u32[]{:S(2)}, u32[]{:S(2)}) collective-permute-start(bf16[64,4096]{1,0:T(8,128)(2,1)} %get-tuple-element.70), channel_id=1, source_target_pairs={{0,8},{4,12},{8,0},{12,4},{16,24},{20,28},{24,16},{28,20},{1,9},{5... | collective-permute-start | bytes 1572872 | tf_op jit(solution)/shard_map/ppermute | solution.py:41
  126.1 43.0 %copy-start.6 = (f32[512]{0:T(512)S(1)}, f32[512]{0:T(512)}, u32[]{:S(2)}) copy-start(f32[512]{0:T(512)} %param.13) | copy-start | bytes 6148
  126.1 43.0 %copy-start.8 = (s32[512]{0:T(512)S(1)}, s32[512]{0:T(512)}, u32[]{:S(2)}) copy-start(s32[512]{0:T(512)} %copy-done.7) | copy-start | bytes 6148
  126.1 21.1 %collective-permute-start.20 = (bf16[64,4096]{1,0:T(8,128)(2,1)S(1)}, bf16[64,4096]{1,0:T(8,128)(2,1)S(1)}, u32[]{:S(2)}, u32[]{:S(2)}) collective-permute-start(bf16[64,4096]{1,0:T(8,128)(2,1)S(1)} %get-tuple-element.72), channel_id=1, source_target_pairs={{0,16},{4,20},{8,24},{12,28},{16,0},{20,4},{24,8},{28,12},{1,17},{... | collective-permute-start | bytes 1572872 | tf_op jit(solution)/shard_map/ppermute | solution.py:41
  127.6 19.6 %collective-permute-start.16 = (bf16[64,4096]{1,0:T(8,128)(2,1)S(1)}, bf16[64,4096]{1,0:T(8,128)(2,1)S(1)}, u32[]{:S(2)}, u32[]{:S(2)}) collective-permute-start(bf16[64,4096]{1,0:T(8,128)(2,1)S(1)} %get-tuple-element.73), channel_id=1, source_target_pairs={{0,8},{4,12},{8,0},{12,4},{16,24},{20,28},{24,16},{28,20},{1,9},{5... | collective-permute-start | bytes 1572872 | tf_op jit(solution)/shard_map/ppermute | solution.py:41
  (1 other events, 3.1 us)
Sparse Core Ops, SparseCore 0:
  94.5 74.5 reduce-scatter.1

commit v4 on v0

v4 whole, which is shorter than its diff:
```python
import math

import jax
import jax.numpy as jnp
from jax import lax
from jax.sharding import PartitionSpec as P

F32 = jnp.float32
BF16 = jnp.bfloat16


def one_hot(index, size):
    return (index[:, None] == jnp.arange(size, dtype=jnp.int32)[None, :]).astype(BF16)


def dot_f32(a, b, dims):
    return lax.dot_general(a, b, (dims, ((), ())), preferred_element_type=F32)


def shift_gather(value, axis, size):
    got = [value]
    for hop in range(1, size):
        got.append(lax.ppermute(value, axis, [(j, (j + hop) % size) for j in range(size)]))
    return got


def swap(value, bit, size):
    return lax.ppermute(value, "dp", [(d, d ^ bit) for d in range(size)])


def after(value, *earlier):
    return lax.optimization_barrier((value, earlier))[0]


def gather_cube(rows):
    half = rows.shape[0] // 2
    over_x = swap(rows, 2, 8)
    over_y = swap(rows, 4, 8)
    over_core = swap(rows, 1, 8)
    first = swap(over_x[:half], 4, 8)
    last = swap(over_y[half:], 2, 8)
    x_core = swap(over_x, 1, 8)
    y_core = swap(over_y, 1, 8)
    far = jnp.concatenate([first, last])
    far_core = swap(far, 1, 8)
    return [rows, over_x, over_y, far, over_core, x_core, y_core, far_core]


def cube_order(index):
    return index ^ jnp.array([0, 2, 4, 6, 1, 3, 5, 7], jnp.int32)


def add_bf16(a, b):
    return (a.astype(F32) + b.astype(F32)).astype(BF16)


def reduce_products(logit_grad, columns, queries, n_dp):
    query_part = dot_f32(logit_grad, columns, ((1,), (0,))).astype(BF16)
    query_grad = lax.psum_scatter(query_part, "neg", scatter_dimension=1, tiled=True)
    logit_grad = after(logit_grad, query_part)
    if n_dp != 8:
        column_part = dot_f32(logit_grad, queries, ((0,), (0,))).astype(BF16)
        column_grad = lax.psum_scatter(column_part, "dp", scatter_dimension=0, tiled=True)
        return query_grad, column_grad
    middle = logit_grad.shape[1] // 2
    room = middle // 4
    half = room // 2
    across = dot_f32(logit_grad[:, middle:], queries, ((0,), (0,))).astype(BF16)
    over_core = swap(across, 1, 8)
    near = dot_f32(after(logit_grad, across)[:, :middle], queries, ((0,), (0,))).astype(BF16)
    total = add_bf16(near, over_core)
    own, to_x, to_y, far = [total[t * room:(t + 1) * room] for t in range(4)]
    far_first = swap(far[:half], 4, 8)
    far_last = swap(far[half:], 2, 8)
    x_last = swap(to_x[half:], 2, 8)
    y_first = swap(to_y[:half], 4, 8)
    x_first = swap(add_bf16(to_x[:half], far_first), 2, 8)
    y_last = swap(add_bf16(to_y[half:], far_last), 4, 8)
    from_x = jnp.concatenate([x_first, x_last])
    from_y = jnp.concatenate([y_first, y_last])
    column_grad = (own.astype(F32) + from_x.astype(F32) + from_y.astype(F32)).astype(BF16)
    return query_grad, column_grad


def gradients(cube, room, queries, passages, counts, rank, pos_id, row_weight, n_dp, n_neg):
    pass_rows, width = passages.shape
    i_dp = lax.axis_index("dp")
    i_neg = lax.axis_index("neg")
    mine = i_dp * n_neg + i_neg
    slots = jnp.arange(room, dtype=jnp.int32)
    own_counts = lax.dynamic_index_in_dim(counts, mine, axis=0, keepdims=False)
    own_rank = lax.dynamic_index_in_dim(rank, mine, axis=0, keepdims=False)
    pick = (
        (own_rank[None, :] == slots[:, None]) & (own_counts[None, :] > 0)
    ).astype(BF16)
    own_rows = dot_f32(pick, passages, ((1,), (0,))).astype(BF16)
    own_rows = lax.optimization_barrier(own_rows)
    if cube:
        blocks = gather_cube(own_rows)
        arrivals = [[0, 4], [1, 2, 5, 6], [3, 7]]
    else:
        blocks = [lax.all_gather(own_rows, "dp", axis=0, tiled=True)]
        arrivals = [[0]]
    columns = jnp.concatenate(blocks)

    order = cube_order(i_dp) if cube else jnp.arange(n_dp, dtype=jnp.int32)
    owner_order = order * n_neg + i_neg
    plane_counts = counts[owner_order]
    plane_rank = rank[owner_order]
    chosen = (plane_rank[:, None, :] == slots[None, :, None]) & (plane_counts[:, None, :] > 0)
    times = jnp.sum(jnp.where(chosen, plane_counts[:, None, :], 0.0), axis=2).reshape(-1)
    names = owner_order[:, None] * pass_rows + jnp.arange(pass_rows, dtype=jnp.int32)[None, :] + 1
    column_id = jnp.sum(jnp.where(chosen, names[:, None, :], 0), axis=2).reshape(-1) - 1
    lift = jnp.where(times > 0, jnp.log(jnp.maximum(times, 1.0)), -1e30)
    target = pos_id[:, None] == column_id[None, :]

    scale = 3.0 / math.sqrt(width)
    factor = row_weight * scale
    lift = lift.reshape(len(blocks), -1)
    logits = [None] * len(blocks)
    for members in arrivals:
        group = jnp.concatenate([blocks[t] for t in members])
        lifts = jnp.concatenate([lift[t] for t in members])
        value = dot_f32(queries, group, ((1,), (1,))) * scale + lifts[None, :]
        for t, part in zip(members, jnp.split(value, len(members), axis=1)):
            logits[t] = part
    logits = jnp.concatenate(logits, axis=1)
    local_max = jnp.max(logits, axis=1)
    expo = jnp.exp(logits - local_max[:, None])
    local_sum = jnp.sum(expo, axis=1)
    stats = shift_gather(jnp.stack([local_max, local_sum]), "neg", n_neg)
    row_max = stats[0][0]
    for other in stats[1:]:
        row_max = jnp.maximum(row_max, other[0])
    row_total = sum(other[1] * jnp.exp(other[0] - row_max) for other in stats)
    share = factor * jnp.exp(local_max - row_max) / row_total
    logit_grad = (
        expo * share[:, None] - jnp.where(target, factor[:, None], 0.0)
    ).astype(BF16)
    logit_grad = lax.optimization_barrier(logit_grad)
    query_grad, column_grad = reduce_products(
        logit_grad, columns, queries, n_dp if cube else 0
    )
    passage_grad = dot_f32(pick, column_grad, ((0,), (0,)))
    return query_grad, passage_grad


def body(n_dp, n_neg, queries, passages, list_owner, list_row, positive, row_weight):
    devices = n_dp * n_neg
    pass_rows = passages.shape[0]
    list_len = list_row.shape[1]
    packed = list_owner.reshape(-1) * pass_rows + list_row.reshape(-1)
    ids = lax.all_to_all(
        jnp.broadcast_to(packed, (devices, list_len)),
        ("neg", "dp"),
        split_axis=0,
        concat_axis=0,
        tiled=True,
    ).reshape(-1)
    owner_of = ids // pass_rows
    row_of = ids % pass_rows
    counts = dot_f32(one_hot(owner_of, devices), one_hot(row_of, pass_rows), ((0,), (0,)))
    present = counts > 0
    order = jnp.arange(pass_rows, dtype=jnp.int32)
    upto = (order[:, None] <= order[None, :]).astype(BF16)
    ends = dot_f32(present.astype(BF16), upto, ((1,), (0,))).astype(jnp.int32)
    rank = ends - 1
    longest = jnp.max(ends)

    high = one_hot(positive // list_len, devices)
    low = one_hot(positive % list_len, list_len).astype(F32)
    owner_table = owner_of.reshape(-1, list_len).astype(BF16)
    row_table = row_of.reshape(-1, list_len).astype(BF16)
    pos_owner = jnp.sum(dot_f32(high, owner_table, ((1,), (0,))) * low, axis=1)
    pos_row = jnp.sum(dot_f32(high, row_table, ((1,), (0,))) * low, axis=1)
    pos_id = pos_owner.astype(jnp.int32) * pass_rows + pos_row.astype(jnp.int32)

    def run(cube, room):
        return lambda: gradients(
            cube, room, queries, passages, counts, rank, pos_id, row_weight, n_dp, n_neg
        )

    return lax.cond(longest <= list_len, run(n_dp == 8, list_len), run(False, pass_rows))


def solution(mesh):
    n_dp, n_neg = mesh.shape["dp"], mesh.shape["neg"]
    in_specs = (
        P("dp", None),
        P(("dp", "neg"), None),
        P("neg", "dp", None),
        P("neg", "dp"),
        P("dp"),
        P("dp"),
    )
    out_specs = (P("dp", "neg"), P(("dp", "neg"), None))

    def run(*args):
        return body(n_dp, n_neg, *args)

    return jax.shard_map(run, mesh=mesh, in_specs=in_specs, out_specs=out_specs, check_vma=False)
```

time: 374 us -> 168 us (0.45); the launches traced: 367 us -> 168 us
  blocking collectives: 189 us -> 0 us
  starting transfers between devices: 0.3 us -> 19.5 us
  waiting for transfers between devices: 113 us -> 98.4 us
  matrix products: 37.5 us -> 26.7 us
    all_to_all x3 -> x0, blocking collectives: 168 us -> none  [the longest x1 105 us: body(): lax.all_to_all(send_slots.reshape(devices, capacity, width).astype(jnp.bf...]
    ppermute x0 -> x18, waiting for transfers between devices: none -> 72.6 us  [the longest x15 67.8 us: swap(): return lax.ppermute(value, 'dp', [(d, d ^ bit) for d in range(size)])]
    all_gather x1 -> x0, waiting for transfers between devices: 54.3 us -> none  [body(): column_block = lax.all_gather(own_rows, 'dp', axis=0, tiled=True)]
    reduce_scatter x2 -> x1, waiting for transfers between devices: 58.5 us -> 19.4 us  [reduce_products(): lax.psum_scatter(query_part, 'neg', scatter_dimension=1, tiled=True)]
    ppermute x0 -> x18, starting transfers between devices: none -> 12.1 us  [the longest x15 9.49 us: swap(): return lax.ppermute(value, 'dp', [(d, d ^ bit) for d in range(size)])]
    pmax x1 -> x0, blocking collectives: 11.8 us -> none  [body(): row_max = lax.pmax(local_max, 'neg')]
    dot_general x6 -> x12, matrix products: 37.5 us -> 26.7 us  [dot_f32(): return lax.dot_general(a, b, (dims, ((), ())), preferred_element_type=F32)]
    psum x1 -> x0, blocking collectives: 8.41 us -> none  [body(): row_total = lax.psum(local_sum * jnp.exp(local_max - row_max), 'neg')]
  transfers between devices with their start and end apart: 3 -> 20, of which waited for: 2 -> 13; matrix products, arithmetic and copies ran while one was open for 6% -> 12% of each run, Pallas kernels for 0% -> 0%
where the time goes in v4:
time: 168 us
  waiting for transfers between devices  98.4 us (59%)
  matrix products  26.7 us (16%)
  starting transfers between devices  19.5 us (12%)
  between operations  14.7 us (9%)
  other arithmetic  4.25 us (3%)
  local copies, waits for them, and re-layouts  3.94 us (2%)
    ppermute x15, waiting for transfers between devices, swap(): return lax.ppermute(value, 'dp', [(d, d ^ bit) for d in range(size)])  67.8 us
    dot_general x12, matrix products, dot_f32(): return lax.dot_general(a, b, (dims, ((), ())), preferred_element_type=F32)  26.7 us
    reduce_scatter x1, waiting for transfers between devices, reduce_products(): lax.psum_scatter(query_part, 'neg', scatter_dimension=1, tiled=True)  19.4 us
    ppermute x15, starting transfers between devices, swap(): return lax.ppermute(value, 'dp', [(d, d ^ bit) for d in range(size)])  9.49 us
    all_to_all x1, starting transfers between devices, body(): lax.all_to_all(jnp.broadcast_to(packed, (devices, list_len)), ('neg', 'dp...  7.3 us
    all_to_all x1, waiting for transfers between devices, body(): lax.all_to_all(jnp.broadcast_to(packed, (devices, list_len)), ('neg', 'dp...  6.38 us
    ppermute x3, waiting for transfers between devices, shift_gather(): lax.ppermute(value, axis, [(j, (j + hop) % size) for j in range(size)])  4.75 us
  transfers between devices with their start and end apart: 20, of which 13 were waited for; matrix products, arithmetic and copies ran while one was open for 12% of the time, Pallas kernels for 0%

profile of v4, /device:TPU:0, one launch (start us, length us, event | category | flops | bytes accessed | tf_op | source)
XLA Modules:
  0.0 168.1 jit_solution(7259347925204363743)
XLA Ops:
  8.5 7.3 %all-to-all-start = ((s32[32,1,128]{2,1,0:T(1,128)}), s32[32,1,128]{2,1,0:T(1,128)S(1)}, u32[]{:S(2)}, u32[]{:S(2)}) async-start(s32[32,1,128]{2,1,0:T(1,128)} %broadcast_in_dim.92), calls=%async_computation.3 | async-start | bytes 32768 | tf_op jit(solution)/shard_map/all_to_all | solution.py:153
  16.5 6.4 %all-to-all-done = s32[32,1,128]{2,1,0:T(1,128)S(1)} async-done(((s32[32,1,128]{2,1,0:T(1,128)}), s32[32,1,128]{2,1,0:T(1,128)S(1)}, u32[]{:S(2)}, u32[]{:S(2)}) %all-to-all-start) | async-done | bytes 16416 | tf_op jit(solution)/shard_map/all_to_all | solution.py:153
  23.5 0.9 fusion.81
  24.4 0.8 broadcast_add_fusion
  25.9 135.4 %conditional.1 = (bf16[512,1024]{1,0:T(8,128)(2,1)}, f32[256,4096]{1,0:T(8,128)}) conditional(s32[]{:T(128)} %convert_element_type.98, (s32[32,256]{1,0:T(8,128)S(1)}, f32[32,256]{1,0:T(8,128)S(1)}, bf16[256,4096]{1,0:T(8,128)(2,1)}, bf16[512,4096]{1,0:T(8,128)(2,1)}, f32[512]{0:T(512)}, /*index=5*/s32[512]{0:T(512)S(1)}) %tuple.18, ...), branch_computations={%region_3.10_spmd, %region_10.21_spmd} | conditional | flops 26875285504 | bytes 221589824 | solution.py:183
  26.2 2.0 %convolution_convert_fusion.6 = bf16[128,4096]{1,0:T(8,128)(2,1)S(1)} fusion(bf16[256,4096]{1,0:T(8,128)(2,1)} %get-tuple-element.35, s32[256]{0:T(256)S(1)} %bitcast.85, pred[256]{0:T(512)(128)(4,1)S(1)} %compare_reduce_fusion.1), kind=kOutput, calls=%fused_computation.41 | convolution fusion | flops 269025280 | bytes 3147008 | tf_op jit(solution)/shard_map/cond/branch_1_fun/dot_general | solution.py:17
  32.1 21.2 %collective-permute-done.5 = bf16[128,4096]{1,0:T(8,128)(2,1)S(1)} collective-permute-done((bf16[128,4096]{1,0:T(8,128)(2,1)S(1)}, bf16[128,4096]{1,0:T(8,128)(2,1)S(1)}, u32[]{:S(2)}, u32[]{:S(2)}) %collective-permute-start.5) | collective-permute-done | bytes 1048608 | tf_op jit(solution)/shard_map/cond/branch_1_fun/ppermute | solution.py:28
  54.0 1.2 collective-permute-start.8
  55.1 2.5 %fusion.56 = f32[512,256]{0,1:T(8,128)S(1)} fusion(bf16[512,4096]{1,0:T(8,128)(2,1)S(1)} %copy-done.2, bf16[128,4096]{1,0:T(8,128)(2,1)} %collective-permute-done.3, bf16[128,4096]{1,0:T(8,128)(2,1)S(1)} %convolution_convert_fusion.6, f32[256]{0:T(256)S(1)} %get-tuple-element.89), kind=kOutput, calls=%fused_computation.72 | convolution fusion | flops 1078198272 | bytes 6816768 | tf_op jit(solution)/shard_map/cond/branch_1_fun/dot_general | solution.py:17
  58.4 7.8 %collective-permute-done.9 = bf16[64,4096]{1,0:T(8,128)(2,1)S(1)} collective-permute-done((bf16[64,4096]{1,0:T(8,128)(2,1)S(1)}, bf16[64,4096]{1,0:T(8,128)(2,1)S(1)}, u32[]{:S(2)}, u32[]{:S(2)}) %collective-permute-start.9) | collective-permute-done | bytes 524320 | tf_op jit(solution)/shard_map/cond/branch_1_fun/ppermute | solution.py:28
  66.8 1.3 constant_dynamic-update-slice_fusion.3
  68.2 2.4 %fusion.38 = f32[512,512]{0,1:T(8,128)S(1)} fusion(bf16[512,4096]{1,0:T(8,128)(2,1)S(1)} %copy-done.2, bf16[128,4096]{1,0:T(8,128)(2,1)S(1)} %collective-permute-done.7, bf16[128,4096]{1,0:T(8,128)(2,1)S(1)} %collective-permute-done.6, bf16[128,4096]{1,0:T(8,128)(2,1)S(1)} %collective-permute-done.5, bf16[128,4096]{1,0:T(8,128)(2,1)S(1)} %collective-permute-done.4, ...), kind=kOutput, calls=%fused_computation.66 | convolution fusion | flops 2164785152 | bytes 9439232 | tf_op jit(solution)/shard_map/cond/branch_1_fun/dot_general | solution.py:17
  70.8 1.3 fusion.50
  73.2 1.6 collective-permute-start.12
  75.4 0.9 collective-permute-done.13
  76.4 1.4 collective-permute-done.12
  77.8 2.5 %collective-permute-done.11 = f32[2,512]{1,0:T(2,128)S(1)} collective-permute-done((f32[2,512]{1,0:T(2,128)S(1)}, f32[2,512]{1,0:T(2,128)S(1)}, u32[]{:S(2)}, u32[]{:S(2)}) %collective-permute-start.11) | collective-permute-done | bytes 4128 | tf_op jit(solution)/shard_map/cond/branch_1_fun/ppermute | solution.py:23
  80.8 6.3 %convolution_convert_fusion.3 = bf16[512,4096]{1,0:T(8,128)(2,1)} fusion(bf16[512,1024]{0,1:T(8,128)(2,1)S(1)} %subtract_convert_fusion, bf16[1024,4096]{1,0:T(8,128)(2,1)S(1)} %constant_dynamic-update-slice_fusion), kind=kOutput, calls=%fused_computation.38 | convolution fusion | flops 4297064448 | bytes 13631488 | tf_op jit(solution)/shard_map/cond/branch_1_fun/dot_general | solution.py:17
  87.1 4.7 %convolution_convert_fusion.5 = bf16[512,4096]{1,0:T(8,128)(2,1)S(1)} fusion(bf16[512,4096]{1,0:T(8,128)(2,1)} %get-tuple-element.36, bf16[512,1024]{0,1:T(8,128)(2,1)S(1)} %subtract_convert_fusion), kind=kOutput, calls=%fused_computation.40 | convolution fusion | flops 2149580800 | bytes 8912896 | tf_op jit(solution)/shard_map/cond/branch_1_fun/dot_general | solution.py:17
  91.9 7.1 %collective-permute-done.14 = bf16[512,4096]{1,0:T(8,128)(2,1)S(1)} collective-permute-done((bf16[512,4096]{1,0:T(8,128)(2,1)S(1)}, bf16[512,4096]{1,0:T(8,128)(2,1)S(1)}, u32[]{:S(2)}, u32[]{:S(2)}) %collective-permute-start.14) | collective-permute-done | bytes 4194336 | tf_op jit(solution)/shard_map/cond/branch_1_fun/ppermute | solution.py:28
  99.1 2.3 %add_convert_fusion = bf16[512,4096]{1,0:T(8,128)(2,1)S(1)} fusion(bf16[512,4096]{1,0:T(8,128)(2,1)S(1)} %collective-permute-done.14, bf16[512,4096]{1,0:T(8,128)(2,1)S(1)} %copy-done.3, bf16[512,1024]{0,1:T(8,128)(2,1)S(1)} %subtract_convert_fusion), kind=kOutput, calls=%fused_computation.37 | convolution fusion | flops 2157969408 | bytes 13107200 | tf_op jit(solution)/shard_map/cond/branch_1_fun/dot_general | solution.py:17
  101.6 1.3 collective-permute-start.19
  103.7 1.3 collective-permute-start.18
  104.9 0.8 collective-permute-start.17
  105.8 10.7 %collective-permute-done.19 = bf16[64,4096]{1,0:T(8,128)(2,1)S(1)} collective-permute-done((bf16[64,4096]{1,0:T(8,128)(2,1)S(1)}, bf16[64,4096]{1,0:T(8,128)(2,1)S(1)}, u32[]{:S(2)}, u32[]{:S(2)}) %collective-permute-start.19) | collective-permute-done | bytes 524320 | tf_op jit(solution)/shard_map/cond/branch_1_fun/ppermute | solution.py:28
  116.5 1.2 collective-permute-done.15
  118.0 0.8 collective-permute-start.20
  118.8 0.8 collective-permute-start.16
  119.6 9.3 %collective-permute-done.18 = bf16[64,4096]{1,0:T(8,128)(2,1)S(1)} collective-permute-done((bf16[64,4096]{1,0:T(8,128)(2,1)S(1)}, bf16[64,4096]{1,0:T(8,128)(2,1)S(1)}, u32[]{:S(2)}, u32[]{:S(2)}) %collective-permute-start.18) | collective-permute-done | bytes 524320 | tf_op jit(solution)/shard_map/cond/branch_1_fun/ppermute | solution.py:28
  128.9 10.1 %collective-permute-done.20 = bf16[64,4096]{1,0:T(8,128)(2,1)S(1)} collective-permute-done((bf16[64,4096]{1,0:T(8,128)(2,1)S(1)}, bf16[64,4096]{1,0:T(8,128)(2,1)S(1)}, u32[]{:S(2)}, u32[]{:S(2)}) %collective-permute-start.20) | collective-permute-done | bytes 524320 | tf_op jit(solution)/shard_map/cond/branch_1_fun/ppermute | solution.py:28
  139.1 2.8 %fusion.59 = f32[256,4096]{1,0:T(8,128)} fusion(bf16[512,4096]{1,0:T(8,128)(2,1)S(1)} %add_convert_fusion, bf16[64,4096]{1,0:T(8,128)(2,1)S(1)} %collective-permute-done.17, bf16[64,4096]{1,0:T(8,128)(2,1)S(1)} %collective-permute-done.16, bf16[64,4096]{1,0:T(8,128)(2,1)S(1)} %collective-permute-done.20, bf16[64,4096]{1,0:T(8,128)(2,1)S(1)} %collective-permute-done.18, ...), kind=kOutput, calls=%fused_computation.73 | convolution fusion | flops 274792448 | bytes 7341568 | tf_op jit(solution)/shard_map/cond/branch_1_fun/dot_general | solution.py:17
  141.9 19.4 %reduce-scatter.8.cloned.1.call-done = bf16[512,1024]{1,0:T(8,128)(2,1)} async-done(((bf16[512,4096]{1,0:T(8,128)(2,1)}), bf16[512,1024]{1,0:T(8,128)(2,1)}) %reduce-scatter.8.cloned.1.call-update) | async-done | bytes 1048592 | tf_op jit(solution)/shard_map/cond/branch_1_fun/reduce_scatter | solution.py:59
  (77 shorter events, 12.4 us)
Async XLA Ops:
  8.5 14.4 %all-to-all-start = ((s32[32,1,128]{2,1,0:T(1,128)}), s32[32,1,128]{2,1,0:T(1,128)S(1)}, u32[]{:S(2)}, u32[]{:S(2)}) async-start(s32[32,1,128]{2,1,0:T(1,128)} %broadcast_in_dim.92), calls=%async_computation.3 | async-start | bytes 32768 | tf_op jit(solution)/shard_map/all_to_all | solution.py:153
  26.1 135.1 %reduce-scatter.8.cloned.1.call-start = ((), (), s32[]{:S(2)}) async-start(), calls=%async_computation.7 | async-start | bytes 5242880 | tf_op jit(solution)/shard_map/cond/branch_1_fun/reduce_scatter | solution.py:59
  28.3 25.0 %collective-permute-start.5 = (bf16[128,4096]{1,0:T(8,128)(2,1)S(1)}, bf16[128,4096]{1,0:T(8,128)(2,1)S(1)}, u32[]{:S(2)}, u32[]{:S(2)}) collective-permute-start(bf16[128,4096]{1,0:T(8,128)(2,1)S(1)} %convolution_convert_fusion.6), channel_id=1, source_target_pairs={{0,16},{4,20},{8,24},{12,28},{16,0},{20,4},{24,8},{28,12},{1,17},{... | collective-permute-start | bytes 3145736 | tf_op jit(solution)/shard_map/cond/branch_1_fun/ppermute | solution.py:28
  28.9 25.0 %collective-permute-start.4 = (bf16[128,4096]{1,0:T(8,128)(2,1)S(1)}, bf16[128,4096]{1,0:T(8,128)(2,1)S(1)}, u32[]{:S(2)}, u32[]{:S(2)}) collective-permute-start(bf16[128,4096]{1,0:T(8,128)(2,1)S(1)} %convolution_convert_fusion.6), channel_id=1, source_target_pairs={{0,8},{4,12},{8,0},{12,4},{16,24},{20,28},{24,16},{28,20},{1,9},{5... | collective-permute-start | bytes 3145736 | tf_op jit(solution)/shard_map/cond/branch_1_fun/ppermute | solution.py:28
  29.5 25.6 %collective-permute-start.3 = (bf16[128,4096]{1,0:T(8,128)(2,1)S(1)}, bf16[128,4096]{1,0:T(8,128)(2,1)}, u32[]{:S(2)}, u32[]{:S(2)}) collective-permute-start(bf16[128,4096]{1,0:T(8,128)(2,1)S(1)} %convolution_convert_fusion.6), channel_id=1, source_target_pairs={{0,4},{4,0},{8,12},{12,8},{16,20},{20,16},{24,28},{28,24},{1,5},{5... | collective-permute-start | bytes 3145736 | tf_op jit(solution)/shard_map/cond/branch_1_fun/ppermute | solution.py:28
  31.3 23.8 %copy-start.2 = (bf16[512,4096]{1,0:T(8,128)(2,1)S(1)}, bf16[512,4096]{1,0:T(8,128)(2,1)}, u32[]{:S(2)}) copy-start(bf16[512,4096]{1,0:T(8,128)(2,1)} %get-tuple-element.36) | copy-start | bytes 12582916 | tf_op jit(solution)/shard_map/cond
  53.3 12.9 %collective-permute-start.9 = (bf16[64,4096]{1,0:T(8,128)(2,1)S(1)}, bf16[64,4096]{1,0:T(8,128)(2,1)S(1)}, u32[]{:S(2)}, u32[]{:S(2)}) collective-permute-start(bf16[64,4096]{1,0:T(8,128)(2,1)S(1)} %slice.149), channel_id=1, source_target_pairs={{0,8},{4,12},{8,0},{12,4},{16,24},{20,28},{24,16},{28,20},{1,9},{5... | collective-permute-start | bytes 1572872 | tf_op jit(solution)/shard_map/cond/branch_1_fun/ppermute | solution.py:28
  54.0 12.6 %collective-permute-start.8 = (bf16[64,4096]{1,0:T(8,128)(2,1)S(1)}, bf16[64,4096]{1,0:T(8,128)(2,1)S(1)}, u32[]{:S(2)}, u32[]{:S(2)}) collective-permute-start(bf16[64,4096]{1,0:T(8,128)(2,1)S(1)} %slice.148), channel_id=1, source_target_pairs={{0,16},{4,20},{8,24},{12,28},{16,0},{20,4},{24,8},{28,12},{1,17},{... | collective-permute-start | bytes 1572872 | tf_op jit(solution)/shard_map/cond/branch_1_fun/ppermute | solution.py:28
  57.7 10.5 %collective-permute-start.7 = (bf16[128,4096]{1,0:T(8,128)(2,1)S(1)}, bf16[128,4096]{1,0:T(8,128)(2,1)S(1)}, u32[]{:S(2)}, u32[]{:S(2)}) collective-permute-start(bf16[128,4096]{1,0:T(8,128)(2,1)S(1)} %collective-permute-done.5), channel_id=1, source_target_pairs={{0,4},{4,0},{8,12},{12,8},{16,20},{20,16},{24,28},{28,24},{1,5},{5... | collective-permute-start | bytes 3145736 | tf_op jit(solution)/shard_map/cond/branch_1_fun/ppermute | solution.py:28
  57.8 10.4 %collective-permute-start.6 = (bf16[128,4096]{1,0:T(8,128)(2,1)S(1)}, bf16[128,4096]{1,0:T(8,128)(2,1)S(1)}, u32[]{:S(2)}, u32[]{:S(2)}) collective-permute-start(bf16[128,4096]{1,0:T(8,128)(2,1)S(1)} %collective-permute-done.4), channel_id=1, source_target_pairs={{0,4},{4,0},{8,12},{12,8},{16,20},{20,16},{24,28},{28,24},{1,5},{5... | collective-permute-start | bytes 3145736 | tf_op jit(solution)/shard_map/cond/branch_1_fun/ppermute | solution.py:28
  66.7 4.1 %collective-permute-start.10 = (bf16[128,4096]{1,0:T(8,128)(2,1)S(1)}, bf16[128,4096]{1,0:T(8,128)(2,1)S(1)}, u32[]{:S(2)}, u32[]{:S(2)}) collective-permute-start(bf16[128,4096]{1,0:T(8,128)(2,1)S(1)} %pad_maximum_fusion.1), channel_id=1, source_target_pairs={{0,4},{4,0},{8,12},{12,8},{16,20},{20,16},{24,28},{28,24},{1,5},{5... | collective-permute-start | bytes 3145736 | tf_op jit(solution)/shard_map/cond/branch_1_fun/ppermute | solution.py:28
  72.1 8.1 %copy-start.1 = (f32[512]{0:T(512)S(1)}, f32[512]{0:T(512)}, u32[]{:S(2)}) copy-start(f32[512]{0:T(512)} %get-tuple-element.38) | copy-start | bytes 6148 | tf_op jit(solution)/shard_map/cond
  72.7 3.7 %collective-permute-start.13 = (f32[2,512]{1,0:T(2,128)S(1)}, f32[2,512]{1,0:T(2,128)S(1)}, u32[]{:S(2)}, u32[]{:S(2)}) collective-permute-start(f32[2,512]{1,0:T(2,128)S(1)} %pad_maximum_fusion.2), channel_id=1, source_target_pairs={{0,3},{1,0},{2,1},{3,2},{4,7},{5,4},{6,5},{7,6},{8,11},{9,8},{10,9... | collective-permute-start | bytes 12296 | tf_op jit(solution)/shard_map/cond/branch_1_fun/ppermute | solution.py:23
  73.2 4.5 %collective-permute-start.12 = (f32[2,512]{1,0:T(2,128)S(1)}, f32[2,512]{1,0:T(2,128)S(1)}, u32[]{:S(2)}, u32[]{:S(2)}) collective-permute-start(f32[2,512]{1,0:T(2,128)S(1)} %pad_maximum_fusion.2), channel_id=1, source_target_pairs={{0,2},{1,3},{2,0},{3,1},{4,6},{5,7},{6,4},{7,5},{8,10},{9,11},{10,... | collective-permute-start | bytes 12296 | tf_op jit(solution)/shard_map/cond/branch_1_fun/ppermute | solution.py:23
  74.8 5.4 %collective-permute-start.11 = (f32[2,512]{1,0:T(2,128)S(1)}, f32[2,512]{1,0:T(2,128)S(1)}, u32[]{:S(2)}, u32[]{:S(2)}) collective-permute-start(f32[2,512]{1,0:T(2,128)S(1)} %pad_maximum_fusion.2), channel_id=1, source_target_pairs={{0,1},{1,2},{2,3},{3,0},{4,5},{5,6},{6,7},{7,4},{8,9},{9,10},{10,1... | collective-permute-start | bytes 12296 | tf_op jit(solution)/shard_map/cond/branch_1_fun/ppermute | solution.py:23
  87.1 12.0 %copy-start.3 = (bf16[512,4096]{1,0:T(8,128)(2,1)S(1)}, bf16[512,4096]{1,0:T(8,128)(2,1)}, u32[]{:S(2)}) copy-start(bf16[512,4096]{1,0:T(8,128)(2,1)} %get-tuple-element.36) | copy-start | bytes 12582916 | tf_op jit(solution)/shard_map/cond
  91.9 7.2 %collective-permute-start.14 = (bf16[512,4096]{1,0:T(8,128)(2,1)S(1)}, bf16[512,4096]{1,0:T(8,128)(2,1)S(1)}, u32[]{:S(2)}, u32[]{:S(2)}) collective-permute-start(bf16[512,4096]{1,0:T(8,128)(2,1)S(1)} %convolution_convert_fusion.5), channel_id=1, source_target_pairs={{0,4},{4,0},{8,12},{12,8},{16,20},{20,16},{24,28},{28,24},{1,5},{5... | collective-permute-start | bytes 12582920 | tf_op jit(solution)/shard_map/cond/branch_1_fun/ppermute | solution.py:28
  101.6 14.8 %collective-permute-start.19 = (bf16[64,4096]{1,0:T(8,128)(2,1)S(1)}, bf16[64,4096]{1,0:T(8,128)(2,1)S(1)}, u32[]{:S(2)}, u32[]{:S(2)}) collective-permute-start(bf16[64,4096]{1,0:T(8,128)(2,1)S(1)} %get-tuple-element.65), channel_id=1, source_target_pairs={{0,8},{4,12},{8,0},{12,4},{16,24},{20,28},{24,16},{28,20},{1,9},{5... | collective-permute-start | bytes 1572872 | tf_op jit(solution)/shard_map/cond/branch_1_fun/ppermute | solution.py:28
  102.9 14.8 %collective-permute-start.15 = (bf16[64,4096]{1,0:T(8,128)(2,1)S(1)}, bf16[64,4096]{1,0:T(8,128)(2,1)S(1)}, u32[]{:S(2)}, u32[]{:S(2)}) collective-permute-start(bf16[64,4096]{1,0:T(8,128)(2,1)S(1)} %get-tuple-element.67), channel_id=1, source_target_pairs={{0,16},{4,20},{8,24},{12,28},{16,0},{20,4},{24,8},{28,12},{1,17},{... | collective-permute-start | bytes 1572872 | tf_op jit(solution)/shard_map/cond/branch_1_fun/ppermute | solution.py:28
  103.7 25.3 %collective-permute-start.18 = (bf16[64,4096]{1,0:T(8,128)(2,1)S(1)}, bf16[64,4096]{1,0:T(8,128)(2,1)S(1)}, u32[]{:S(2)}, u32[]{:S(2)}) collective-permute-start(bf16[64,4096]{1,0:T(8,128)(2,1)S(1)} %get-tuple-element.64), channel_id=1, source_target_pairs={{0,16},{4,20},{8,24},{12,28},{16,0},{20,4},{24,8},{28,12},{1,17},{... | collective-permute-start | bytes 1572872 | tf_op jit(solution)/shard_map/cond/branch_1_fun/ppermute | solution.py:28
  104.9 24.0 %collective-permute-start.17 = (bf16[64,4096]{1,0:T(8,128)(2,1)S(1)}, bf16[64,4096]{1,0:T(8,128)(2,1)S(1)}, u32[]{:S(2)}, u32[]{:S(2)}) collective-permute-start(bf16[64,4096]{1,0:T(8,128)(2,1)S(1)} %get-tuple-element.66), channel_id=1, source_target_pairs={{0,8},{4,12},{8,0},{12,4},{16,24},{20,28},{24,16},{28,20},{1,9},{5... | collective-permute-start | bytes 1572872 | tf_op jit(solution)/shard_map/cond/branch_1_fun/ppermute | solution.py:28
  118.0 21.1 %collective-permute-start.20 = (bf16[64,4096]{1,0:T(8,128)(2,1)S(1)}, bf16[64,4096]{1,0:T(8,128)(2,1)S(1)}, u32[]{:S(2)}, u32[]{:S(2)}) collective-permute-start(bf16[64,4096]{1,0:T(8,128)(2,1)S(1)} %get-tuple-element.68), channel_id=1, source_target_pairs={{0,16},{4,20},{8,24},{12,28},{16,0},{20,4},{24,8},{28,12},{1,17},{... | collective-permute-start | bytes 1572872 | tf_op jit(solution)/shard_map/cond/branch_1_fun/ppermute | solution.py:28
  118.8 20.3 %collective-permute-start.16 = (bf16[64,4096]{1,0:T(8,128)(2,1)S(1)}, bf16[64,4096]{1,0:T(8,128)(2,1)S(1)}, u32[]{:S(2)}, u32[]{:S(2)}) collective-permute-start(bf16[64,4096]{1,0:T(8,128)(2,1)S(1)} %get-tuple-element.69), channel_id=1, source_target_pairs={{0,8},{4,12},{8,0},{12,4},{16,24},{20,28},{24,16},{28,20},{1,9},{5... | collective-permute-start | bytes 1572872 | tf_op jit(solution)/shard_map/cond/branch_1_fun/ppermute | solution.py:28
Sparse Core Ops, SparseCore 0:
  87.2 74.0 reduce-scatter.7
